TPU v7x, 128 devices: a whole 4x4x4 slice. The times are simulated.
128 devices in a mesh: dp: 8 (over z, y_lo), mp: 16 (over y_hi, x, core).
Axes of the slice: x: 4, y: 4 (y_hi: 2, y_lo: 2; y = y_hi * 2 + y_lo), z: 4, core: 2. Of those that a mesh axis runs over, the one named last changes fastest.
Arguments:
- edge_feats: bfloat16 [32768, 3072], P(('dp', 'mp')), may hold values from -6 to 6
- targets: int32 [32768], P(('dp', 'mp')), may hold values from 0 to 127
- roll_ids: int32 [32768], P(('dp', 'mp')), may hold values from 0 to 63
- counts: int32 [128], P(('dp', 'mp')), may hold values from 32 to 256, as said below
- coefs: float32 [8, 16], replicated, may hold values from 0.05 to 0.45
- weights: bfloat16 [16, 1536, 2, 1536], P(None, 'mp'), may hold values from -0.109375 to 0.109375
- roll_angles: float32 [64], replicated, may hold values from -3.140625 to 3.140625
- atom_cot: bfloat16 [1024, 3072], P(('dp', 'mp')), may hold values from -16 to 16
Outputs:
- atom_out: bfloat16 [1024, 3072], P(('dp', 'mp'))
- edge_grad: bfloat16 [32768, 3072], P(('dp', 'mp'))
- weight_grad: bfloat16 [16, 1536, 2, 1536], P(None, 'mp')
- coef_grad: float32 [8, 16], P('dp')
Inputs may be any that keep to these rules, and one draw needn't show every extreme that they name: `counts`: some device uses all 256 slots in every draw.
All inputs are finite; a program needn't handle non-finite values.
Results may differ from a plain program's by a relative error of at most 0.023.
Values may be sent and summed in bfloat16 or wider, within the bound.
A program may use at most 128 MiB of HBM per device.

v0:
```python
import jax
import jax.numpy as jnp
from jax import lax
from jax.sharding import PartitionSpec as P


def on_device(edge_feats, targets, roll_ids, counts, coefs, weights, roll_angles, atom_cot):
    highest = lax.Precision.HIGHEST
    slots = edge_feats.shape[0]
    width = weights.shape[3]
    atoms_here = atom_cot.shape[0]
    group_size = lax.axis_size("mp")
    scale = (atoms_here / slots) ** 0.5
    grad_norm = (slots * group_size) ** (-0.5)
    crystal = lax.axis_index("dp")
    coef_row = lax.dynamic_slice_in_dim(coefs, crystal, 1, 0)[0]
    merged = jnp.einsum(
        "k,krab->rab", coef_row, weights, precision=highest, preferred_element_type=jnp.float32
    ).astype(jnp.bfloat16)
    valid = (jnp.arange(slots) < counts[0]).astype(jnp.float32)[:, None]
    factor = scale * valid
    table_hits = (roll_ids[:, None] == jnp.arange(roll_angles.shape[0])[None, :]).astype(
        jnp.float32
    )
    angles = jnp.dot(table_hits, roll_angles, precision=highest)[:, None]
    cosine, sine = (jnp.cos(angles), jnp.sin(angles))
    plus_in, minus_in = (edge_feats[:, :width], edge_feats[:, width:])
    row_contract = (((1,), (1,)), ((), ()))
    slot_contract = (((0,), (0,)), ((), ()))
    piece = lax.all_gather(atom_cot, "mp", axis=0, tiled=True)
    hits = (targets[:, None] == jnp.arange(piece.shape[0])[None, :]).astype(jnp.bfloat16)
    cot_edges = jnp.dot(hits, piece, preferred_element_type=jnp.float32) * factor
    cot_plus, cot_minus = (cot_edges[:, :width], cot_edges[:, width:])
    grad_plus = (cosine * cot_plus + sine * cot_minus).astype(jnp.bfloat16)
    grad_minus = (cosine * cot_minus - sine * cot_plus).astype(jnp.bfloat16)
    piece = lax.all_gather(merged, "mp", axis=0, tiled=True)
    plus_cols = plus_in
    minus_cols = minus_in
    real_part = piece[:, 0, :]
    imag_part = piece[:, 1, :]
    out_plus = jnp.dot(plus_cols, real_part, preferred_element_type=jnp.float32) - jnp.dot(
        minus_cols, imag_part, preferred_element_type=jnp.float32
    )
    out_minus = jnp.dot(plus_cols, imag_part, preferred_element_type=jnp.float32) + jnp.dot(
        minus_cols, real_part, preferred_element_type=jnp.float32
    )
    out_plus, out_minus = (out_plus, out_minus)
    piece = lax.all_gather(merged, "mp", axis=0, tiled=True)
    real_part = piece[:, 0, :]
    imag_part = piece[:, 1, :]
    back_plus = lax.dot_general(
        grad_plus, real_part, row_contract, preferred_element_type=jnp.float32
    ) + lax.dot_general(grad_minus, imag_part, row_contract, preferred_element_type=jnp.float32)
    back_minus = lax.dot_general(
        grad_minus, real_part, row_contract, preferred_element_type=jnp.float32
    ) - lax.dot_general(grad_plus, imag_part, row_contract, preferred_element_type=jnp.float32)
    backed = jnp.stack([back_plus, back_minus], 1)
    edge_grad = backed.reshape(slots, 2 * width).astype(jnp.bfloat16)
    rolled = jnp.concatenate(
        [
            (cosine * out_plus - sine * out_minus) * factor,
            (sine * out_plus + cosine * out_minus) * factor,
        ],
        1,
    )
    hits = (targets[:, None] == jnp.arange(lax.axis_size("mp") * atoms_here)[None, :]).astype(
        jnp.float32
    )
    atom_out = lax.psum_scatter(
        lax.dot_general(hits, rolled, slot_contract, precision=highest).astype(jnp.bfloat16),
        "mp",
        scatter_dimension=0,
        tiled=True,
    )
    plus_cols = plus_in
    minus_cols = minus_in
    d_real = lax.dot_general(
        plus_cols, grad_plus, slot_contract, preferred_element_type=jnp.float32
    ) + lax.dot_general(minus_cols, grad_minus, slot_contract, preferred_element_type=jnp.float32)
    d_imag = lax.dot_general(
        plus_cols, grad_minus, slot_contract, preferred_element_type=jnp.float32
    ) - lax.dot_general(minus_cols, grad_plus, slot_contract, preferred_element_type=jnp.float32)
    rounded = (jnp.stack([d_real, d_imag], 1) * grad_norm).astype(jnp.bfloat16)
    grad_rows = lax.psum_scatter(
        lax.optimization_barrier(rounded).astype(jnp.float32).astype(jnp.bfloat16),
        "mp",
        scatter_dimension=0,
        tiled=True,
    ).astype(jnp.float32)
    weight_sum = jnp.zeros((weights.shape[0],) + grad_rows.shape, jnp.float32) + jnp.einsum(
        "ck,crab->krab",
        coefs,
        lax.all_gather(grad_rows[None].astype(jnp.bfloat16), "dp", axis=0, tiled=True).astype(
            jnp.float32
        ),
        precision=highest,
    )
    weight_grad = weight_sum.astype(jnp.bfloat16)
    local_coef = jnp.einsum(
        "krab,rab->k", weights, grad_rows, precision=highest, preferred_element_type=jnp.float32
    )
    coef_grad = (lax.psum(local_coef, "mp") / width**0.5)[None, :]
    return (atom_out, edge_grad, weight_grad, coef_grad)


def solution(mesh):
    placed = (
        P(("dp", "mp"), None),
        P(("dp", "mp")),
        P(("dp", "mp")),
        P(("dp", "mp")),
        P(),
        P(None, "mp", None, None),
        P(),
        P(("dp", "mp"), None),
    )
    return jax.shard_map(
        on_device,
        mesh=mesh,
        in_specs=placed,
        out_specs=(
            P(("dp", "mp"), None),
            P(("dp", "mp"), None),
            P(None, "mp", None, None),
            P("dp", None),
        ),
        check_vma=False,
    )
```

profile of v0, /device:TPU:1, one launch (start us, length us, event | category | flops | bytes accessed | tf_op | source)
XLA Modules:
  0.0 495.2 jit_solution(15229899015182476590)
XLA Ops:
  7.9 28.1 %all_gather.11 = bf16[128,3072]{1,0:T(8,128)(2,1)S(1)} all-gather(bf16[8,3072]{1,0:T(8,128)(2,1)} %param.15), channel_id=1, replica_groups=mesh['dp'=8,'mp'=16] {'mp'}, dimensions={0}, use_global_device_ids=true | all-gather | bytes 835584 | tf_op jit(solution)/shard_map/all_gather | solution.py:30
  36.9 1.3 convolution_multiply_fusion
  39.6 1.4 fusion.39
  41.0 1.4 fusion.37
  42.5 1.5 fusion.5
  43.9 1.5 fusion.6
  45.4 5.0 %fusion = bf16[1536,2,1536]{0,2,1:T(8,128)(2,1)} fusion(f32[1536,1,1536]{0,2,1:T(8,128)S(1)} %fusion.6, f32[1536,1,1536]{0,2,1:T(8,128)S(1)} %fusion.5), kind=kLoop, calls=%fused_computation.1 | loop fusion | flops 14155776 | bytes 28311552 | tf_op jit(solution)/shard_map/convert_element_type | solution.py:83
  50.4 24.1 %copy.20 = bf16[1536,2,1536]{2,1,0:T(2,128)(2,1)} copy(bf16[1536,2,1536]{0,2,1:T(8,128)(2,1)} %fusion) | data formatting | bytes 18874368 | tf_op jit(solution)/shard_map/optimization_barrier | solution.py:85
  75.1 12.6 %fusion.3 = bf16[1,96,2,1536]{3,0,2,1:T(2,128)(2,1)S(1)} fusion(bf16[16,96,2,1536]{3,2,1,0:T(2,128)(2,1)} %param.13, f32[8,16]{1,0:T(8,128)S(1)} %copy-done, s32[]{:T(128)S(6)} %select_n.3), kind=kOutput, calls=%fused_computation.6 | convolution fusion | flops 56623104 | bytes 10027524 | tf_op jit(solution)/shard_map/k,krab->rab/dot_general | solution.py:17
  87.7 1.0 copy.47
  90.0 147.5 %all-reduce.3.cloned.1.call-done = bf16[1536,2,1536]{2,1,0:T(2,128)(2,1)} async-done(((bf16[1536,2,1536]{2,1,0:T(2,128)(2,1)}), bf16[1536,2,1536]{2,1,0:T(2,128)(2,1)}) %all-reduce.3.cloned.1.call-update) | async-done | bytes 9437200
  237.5 2.3 constant_dynamic-slice_fusion
  239.9 1.5 fusion.67
  241.3 10.0 %fusion.28 = f32[16]{0:T(128)S(1)} fusion(bf16[16,96,2,1536]{3,2,1,0:T(2,128)(2,1)} %param.13, bf16[96,2,1536,1]{2,1,0,3:T(2,128)(2,1)S(1)} %fusion.67), kind=kOutput, calls=%fused_computation.42 | convolution fusion | flops 9437184 | bytes 10027072 | tf_op jit(solution)/shard_map/krab,rab->k/dot_general | solution.py:99
  251.3 35.3 %psum.7 = f32[16]{0:T(128)S(1)} all-reduce(f32[16]{0:T(128)S(1)} %fusion.28), channel_id=1, replica_groups=mesh['dp'=8,'mp'=16] {'mp'}, use_global_device_ids=true, to_apply=%region_2.0 | all-reduce | flops 16 | bytes 128 | tf_op jit(solution)/shard_map/psum | solution.py:102
  287.1 32.8 %all-gather.4.cloned.1.call-done = bf16[1536,2,1536]{2,0,1:T(8,128)(2,1)} async-done(((bf16[96,2,1536]{2,0,1:T(8,128)(2,1)}), bf16[1536,2,1536]{2,0,1:T(8,128)(2,1)}) %all-gather.4.cloned.1.call-update) | async-done | bytes 9437200 | tf_op jit(solution)/shard_map/all_gather | solution.py:36
  320.0 4.0 fusion.13
  324.0 1.1 copy-done.3
  325.1 1.5 fusion.14
  326.6 1.5 fusion.19
  328.1 1.9 multiply_bitcast_fusion.1
  330.0 2.8 convolution_convert_fusion
  332.9 3.9 fusion.12
  336.8 3.9 fusion.11
  340.7 1.5 fusion.25
  342.2 1.5 fusion.26
  343.8 0.9 copy.19
  344.7 1.7 copy.23
  346.4 73.6 %all-gather.6.cloned.1.call-done = bf16[768,2,1536]{2,1,0:T(2,128)(2,1)} async-done(((bf16[96,2,1536]{2,1,0:T(2,128)(2,1)}), bf16[768,2,1536]{2,1,0:T(2,128)(2,1)}) %all-gather.6.cloned.1.call-update) | async-done | bytes 4718608 | tf_op jit(solution)/shard_map/all_gather | solution.py:93
  420.1 10.7 %convert_bitcast_fusion = bf16[16,96,2,1536]{3,0,2,1:T(8,128)(2,1)S(1)} fusion(bf16[8,96,2,1536]{3,2,1,0:T(2,128)(2,1)} %bitcast.90, f32[8,16]{1,0:T(8,128)S(1)} %copy-done), kind=kOutput, calls=%fused_computation.8 | convolution fusion | flops 457703424 | bytes 14156288 | tf_op jit(solution)/shard_map/ck,crab->krab/dot_general | solution.py:90
  430.8 36.3 %copy.24 = bf16[16,96,2,1536]{3,2,1,0:T(2,128)(2,1)} copy(bf16[16,96,2,1536]{3,0,2,1:T(8,128)(2,1)S(1)} %convert_bitcast_fusion) | data formatting | bytes 18874368
  467.1 21.3 %reduce-scatter.2.cloned.1.call-done = bf16[8,3072]{1,0:T(8,128)(2,1)} async-done(((bf16[128,3072]{1,0:T(8,128)(2,1)}), bf16[8,3072]{1,0:T(8,128)(2,1)}) %reduce-scatter.2.cloned.1.call-update) | async-done | bytes 49168 | tf_op jit(solution)/shard_map/reduce_scatter | solution.py:69
  (30 shorter events, 4.4 us)
Async XLA Ops:
  7.2 67.9 %copy-start = (f32[8,16]{1,0:T(8,128)S(1)}, f32[8,16]{1,0:T(8,128)}, u32[]{:S(2)}) copy-start(f32[8,16]{1,0:T(8,128)} %param.12) | copy-start | bytes 1540
  7.2 230.3 %all-reduce.3.cloned.1.call-start = ((), (), s32[]{:S(2)}) async-start(), calls=%async_computation.4 | async-start | bytes 18874368
  38.2 1.4 copy-start.1
  74.6 245.4 %all-gather.4.cloned.1.call-start = ((), (), s32[]{:S(2)}) async-start(), calls=%async_computation.1 | async-start | bytes 10027008 | tf_op jit(solution)/shard_map/all_gather | solution.py:36
  75.1 13.7 %copy-start.4 = (u32[128]{0:T(128)S(1)}, u32[128]{0:T(128)}, u32[]{:S(2)}) copy-start(u32[128]{0:T(128)} %constant.23) | copy-start | bytes 1540
  88.7 331.4 %all-gather.6.cloned.1.call-start = ((), (), s32[]{:S(2)}) async-start(), calls=%async_computation.3 | async-start | bytes 5308416 | tf_op jit(solution)/shard_map/all_gather | solution.py:93
  239.8 248.6 %reduce-scatter.2.cloned.1.call-start = ((), (), s32[]{:S(2)}) async-start(), calls=%async_computation.2 | async-start | bytes 835584 | tf_op jit(solution)/shard_map/reduce_scatter | solution.py:69
  320.0 5.1 %copy-start.3 = (bf16[1536,2,1536]{2,0,1:T(8,128)(2,1)S(1)}, bf16[1536,2,1536]{2,0,1:T(8,128)(2,1)}, u32[]{:S(2)}) copy-start(bf16[1536,2,1536]{2,0,1:T(8,128)(2,1)} %all-gather.4.cloned.1.call-done) | copy-start | bytes 28311556
  328.1 1.9 copy-start.2
  332.8 7.8 %slice-start = ((s8[9437184]{0:T(1024)(128)(4,1)}), s8[4194304]{0:T(1024)(128)(4,1)S(1)}, s32[]{:S(2)}) async-start(s8[9437184]{0:T(1024)(128)(4,1)} %bitcast.93), calls=%async_computation.5 | async-start | bytes 8388608
  332.8 7.8 %slice-start.1 = ((s8[9437184]{0:T(1024)(128)(4,1)}), s8[4194304]{0:T(1024)(128)(4,1)S(1)}, s32[]{:S(2)}) async-start(s8[9437184]{0:T(1024)(128)(4,1)} %bitcast.93), calls=%async_computation.6 | async-start | bytes 8388608
  336.8 3.9 slice-start.2
Sparse Core Ops, SparseCore 0:
  74.7 162.7 all-reduce.2
  240.6 79.3 all-gather.3
  322.2 97.8 all-gather.5
  424.3 64.1 reduce-scatter.1
where the time goes:
time: 503 us; the launch traced here: 495 us
  waiting for transfers between devices  275 us (55%)
  local copies, waits for them, and re-layouts  70.4 us (14%)
  matrix products  63.5 us (13%)
  blocking collectives  63.3 us (13%)
  between operations  15.6 us (3%)
  other arithmetic  6.45 us (1%)
    unnamed x5, waiting for transfers between devices  148 us
    all_gather x1, waiting for transfers between devices, on_device(): lax.all_gather(grad_rows[None].astype(jnp.bfloat16), 'dp', axis=0, tiled=...  73.6 us
    unnamed x20, local copies, waits for them, and re-layouts  42.8 us
    psum x1, blocking collectives, on_device(): coef_grad = (lax.psum(local_coef, 'mp') / width ** 0.5)[None, :]  35.3 us
    all_gather x1, waiting for transfers between devices, on_device(): piece = lax.all_gather(merged, 'mp', axis=0, tiled=True)  32.8 us
    all_gather x1, blocking collectives, on_device(): piece = lax.all_gather(atom_cot, 'mp', axis=0, tiled=True)  28.1 us
    optimization_barrier x1, local copies, waits for them, and re-layouts, on_device(): lax.optimization_barrier(rounded).astype(jnp.float32).astype(jnp.bfloat16)  24.1 us
    reduce_scatter x1, waiting for transfers between devices, on_device(): lax.psum_scatter(lax.dot_general(hits, rolled, slot_contract, precision=h...  21.3 us
  transfers between devices with their start and end apart: 4, of which 4 were waited for; matrix products, arithmetic and copies ran while one was open for 20% of the time, Pallas kernels for 0%

commit v1 on v0

v1 whole, which is shorter than its diff:
```python
import functools

import jax
import jax.numpy as jnp
from jax import lax
from jax.experimental import pallas as pl
from jax.experimental.pallas import tpu as pltpu
from jax.sharding import PartitionSpec as P

BF16, F32 = jnp.bfloat16, jnp.float32
LANES = 128


def dot(a, b, contract):
    return lax.dot_general(a, b, (contract, ((), ())), preferred_element_type=F32)


def turn(rows):
    n = rows.shape[1]
    col = lax.broadcasted_iota(jnp.int32, rows.shape, 1)
    return jnp.where(col // 8 % 2 == 0, jnp.roll(rows, -8, 1), -jnp.roll(rows, 8, 1))


def mix_kernel(experts, crystals, norm, steps, coefs_ref, x_ref, cot_ref, back_ref, spread_ref, wg_ref, eg_ref,
               gm_ref, flat_ref, left_ref):
    step = pl.program_id(0)
    rows = x_ref.shape[1]
    width = cot_ref.shape[2]
    tiles = width // LANES

    @pl.when(step == 0)
    def _():
        r = lax.broadcasted_iota(jnp.int32, (16 * experts, 16 * crystals), 0)
        c = lax.broadcasted_iota(jnp.int32, (16 * experts, 16 * crystals), 1)
        mixed = jnp.zeros((16 * experts, 16 * crystals), F32)
        for k in range(experts):
            for i in range(crystals):
                mixed = jnp.where((r // 16 == k) & (c // 16 == i), coefs_ref[i, k], mixed)
        mixed = jnp.where(r % 16 == c % 16, mixed, 0.0)
        high = mixed.astype(BF16)
        left_ref[:, : 16 * crystals] = high
        left_ref[:, 16 * crystals :] = (mixed - high.astype(F32)).astype(BF16)
        for i in range(crystals):
            x = x_ref[i].astype(F32)
            both = jnp.concatenate([x, -turn(x)], 0).astype(BF16)
            for t in range(tiles):
                grad = dot(both, cot_ref[i, :, t * LANES : (t + 1) * LANES], ((1,), (0,))) * norm
                for part in range(2):
                    flat_ref[pl.ds(t * 2 + part, rows, stride=2 * tiles), :] = grad[part * rows : (part + 1) * rows]
            gm_ref[i] = flat_ref[...].astype(BF16)

    chunk = wg_ref.shape[1]
    for pair in range(chunk // 32):
        start = pl.multiple_of(step * chunk + pair * 32, 32)
        first = [gm_ref[i, pl.ds(start, 16), :] for i in range(crystals)]
        second = [gm_ref[i, pl.ds(start + 16, 16), :] for i in range(crystals)]
        right = jnp.concatenate([jnp.concatenate(first * 2, 0), jnp.concatenate(second * 2, 0)], 1)
        out = dot(left_ref[...], right, ((1,), (0,))).astype(BF16)
        for k in range(experts):
            wg_ref[k, pair * 32 : pair * 32 + 16, :] = out[k * 16 : (k + 1) * 16, :LANES]
            wg_ref[k, pair * 32 + 16 : pair * 32 + 32, :] = out[k * 16 : (k + 1) * 16, LANES:]
    part = step // (steps // 2)
    cols = eg_ref.shape[1]
    at = pl.multiple_of(step % (steps // 2) * cols, cols)
    eg_ref[...] = dot(spread_ref[part], back_ref[pl.ds(at, cols), :], ((1,), (1,))).astype(BF16)


def mix(coefs, x_all, cot_all, back_all, spread, norm):
    crystals, experts = coefs.shape
    _, rows, q = x_all.shape
    width = cot_all.shape[2]
    flat = rows * 2 * width // LANES
    slots = spread.shape[1]
    steps = 12
    whole = lambda shape: pl.BlockSpec(shape, lambda i: (0,) * len(shape))
    return pl.pallas_call(
        functools.partial(mix_kernel, experts, crystals, norm, steps),
        grid=(steps,),
        in_specs=[
            pl.BlockSpec(memory_space=pltpu.SMEM),
            whole(x_all.shape),
            whole(cot_all.shape),
            whole(back_all.shape),
            whole(spread.shape),
        ],
        out_specs=[
            pl.BlockSpec((experts, flat // steps, LANES), lambda i: (0, i, 0)),
            pl.BlockSpec((slots, 2 * width // steps), lambda i: (0, i)),
        ],
        out_shape=[
            jax.ShapeDtypeStruct((experts, flat, LANES), BF16),
            jax.ShapeDtypeStruct((slots, 2 * width), BF16),
        ],
        scratch_shapes=[
            pltpu.VMEM((crystals, flat, LANES), BF16),
            pltpu.VMEM((flat, LANES), F32),
            pltpu.VMEM((16 * experts, 32 * crystals), BF16),
        ],
        compiler_params=pltpu.CompilerParams(vmem_limit_bytes=48 * 2**20),
        cost_estimate=pl.CostEstimate(flops=10**10, bytes_accessed=2 * 10**7, transcendentals=0),
    )(coefs, x_all, cot_all, back_all, spread)


def on_device(edge_feats, targets, roll_ids, counts, coefs, weights, roll_angles, atom_cot):
    highest = lax.Precision.HIGHEST
    slots = edge_feats.shape[0]
    experts, rows, _, width = weights.shape
    atoms_here = atom_cot.shape[0]
    group, crystals = lax.axis_size("mp"), lax.axis_size("dp")
    q = 2 * group * atoms_here
    scale = (atoms_here / slots) ** 0.5
    norm = (slots * group) ** (-0.5)
    crystal = lax.axis_index("dp")
    cot_rows = jnp.concatenate([atom_cot[:, :width], atom_cot[:, width:]], 0)
    cot_all = lax.all_gather(cot_rows, ("dp", "mp"), axis=0, tiled=True).reshape(crystals, q, width)
    cot = lax.dynamic_index_in_dim(cot_all, crystal, 0, False)

    coef_row = lax.dynamic_slice_in_dim(coefs, crystal, 1, 0)[0]
    flat = weights.reshape(experts, rows, 2, width // LANES, LANES).transpose(0, 1, 3, 2, 4)
    flat = flat.reshape(experts, rows * 2 * width // LANES, LANES)
    merged = jnp.sum(coef_row[:, None, None] * flat.astype(F32), 0).astype(BF16)
    merged = merged.reshape(rows, width // LANES, 2, LANES).transpose(2, 0, 1, 3).reshape(2 * rows, width)

    factor = scale * (jnp.arange(slots) < counts[0]).astype(F32)[:, None]
    cosine = (jnp.cos(roll_angles)[roll_ids])[:, None] * factor
    sine = (jnp.sin(roll_angles)[roll_ids])[:, None] * factor
    col = jnp.arange(q)[None, :]
    hit = targets[:, None] == col // 16 * 8 + col % 8
    real = col // 8 % 2 == 0
    spread_plus = jnp.where(hit, jnp.where(real, cosine, sine), 0.0).astype(BF16)
    spread_minus = jnp.where(hit, jnp.where(real, -sine, cosine), 0.0).astype(BF16)

    x_part = dot(edge_feats[:, :width], spread_plus, ((0,), (0,))) + dot(
        edge_feats[:, width:], spread_minus, ((0,), (0,))
    )
    x_here = lax.psum_scatter(x_part.astype(BF16), "mp", scatter_dimension=0, tiled=True)
    x_all = lax.all_gather(x_here[None], "dp", axis=0, tiled=True)
    x_wide = x_here.astype(F32)
    both = jnp.concatenate([x_wide, -turn(x_wide)], 0).astype(BF16)
    out_part = dot(both, merged, ((0,), (0,)))
    out = lax.psum_scatter(out_part.astype(BF16), "mp", scatter_dimension=0, tiled=True)
    atom_out = jnp.concatenate([out[:atoms_here], out[atoms_here:]], 1)

    back = dot(merged, cot, ((1,), (1,)))
    back = (back[:rows] + turn(back[rows:])).astype(BF16)
    back_all = lax.all_gather(back, "mp", axis=0, tiled=True)

    grad = dot(both, cot, ((1,), (0,))) * norm
    grad_flat = grad.reshape(2, rows, width // LANES, LANES).transpose(1, 2, 0, 3).reshape(-1, LANES)
    local_coef = jnp.sum(flat.astype(F32) * grad_flat[None], (1, 2))
    coef_grad = (lax.psum(local_coef, "mp") / width**0.5)[None, :]

    wg, edge_grad = mix(coefs, x_all, cot_all, back_all, jnp.stack([spread_plus, spread_minus]), norm)
    weight_grad = wg.reshape(experts, rows, width // LANES, 2, LANES).transpose(0, 1, 3, 2, 4)
    weight_grad = weight_grad.reshape(weights.shape)
    return (atom_out, edge_grad, weight_grad, coef_grad)


def solution(mesh):
    placed = (
        P(("dp", "mp"), None),
        P(("dp", "mp")),
        P(("dp", "mp")),
        P(("dp", "mp")),
        P(),
        P(None, "mp", None, None),
        P(),
        P(("dp", "mp"), None),
    )
    return jax.shard_map(
        on_device,
        mesh=mesh,
        in_specs=placed,
        out_specs=(
            P(("dp", "mp"), None),
            P(("dp", "mp"), None),
            P(None, "mp", None, None),
            P("dp", None),
        ),
        check_vma=False,
    )
```

time: 503 us -> 372 us (0.74); the launches traced: 495 us -> 370 us
  waiting for transfers between devices: 275 us -> 146 us
  matrix products: 63.5 us -> 6.46 us
  local copies, waits for them, and re-layouts: 70.4 us -> 90.4 us
  blocking collectives: 63.3 us -> 82.5 us
  Pallas kernels: 0 us -> 14.4 us
  other arithmetic: 6.45 us -> 14.5 us
    unnamed x5 -> x3, waiting for transfers between devices: 148 us -> 0.05 us
    dot_general x18 -> x5, matrix products: 63.5 us -> 6.46 us  [dot(): lax.dot_general(a, b, (contract, ((), ())), preferred_element_type=F32)]
    convert_element_type x0 -> x2, local copies, waits for them, and re-layouts: none -> 36 us  [on_device(): merged = jnp.sum(coef_row[:, None, None] * flat.astype(F32), 0).astype(BF16)]
    reshape x0 -> x3, local copies, waits for them, and re-layouts: none -> 28.7 us  [the longest x1 17.8 us: on_device(): weight_grad = weight_grad.reshape(weights.shape)]
    unnamed x20 -> x11, local copies, waits for them, and re-layouts: 42.8 us -> 18.4 us
    optimization_barrier x1 -> x0, local copies, waits for them, and re-layouts: 24.1 us -> none  [on_device(): lax.optimization_barrier(rounded).astype(jnp.float32).astype(jnp.bfloat16)]
    all_gather x1 -> x2, blocking collectives: 28.1 us -> 49.8 us  [the longest x1 25.4 us: on_device(): back_all = lax.all_gather(back, 'mp', axis=0, tiled=True)]
    pallas_call x0 -> x1, Pallas kernels: none -> 14.4 us  [mix(): pl.pallas_call(functools.partial(mix_kernel, experts, crystals, norm, ste...]
  transfers between devices with their start and end apart: 4 -> 3, of which waited for: 4 -> 2; matrix products, arithmetic and copies ran while one was open for 20% -> 23% of each run, Pallas kernels for 0% -> 4%
where the time goes in v1:
time: 372 us; the launch traced here: 370 us
  waiting for transfers between devices  146 us (39%)
  local copies, waits for them, and re-layouts  90.4 us (24%)
  blocking collectives  82.5 us (22%)
  between operations  16.3 us (4%)
  other arithmetic  14.5 us (4%)
  Pallas kernels  14.4 us (4%)
  matrix products  6.46 us (2%)
    all_gather x1, waiting for transfers between devices, on_device(): lax.all_gather(cot_rows, ('dp', 'mp'), axis=0, tiled=True)  115 us
    convert_element_type x2, local copies, waits for them, and re-layouts, on_device(): merged = jnp.sum(coef_row[:, None, None] * flat.astype(F32), 0).astype(BF16)  36 us
    psum x1, blocking collectives, on_device(): coef_grad = (lax.psum(local_coef, 'mp') / width ** 0.5)[None, :]  32.6 us
    reduce_scatter x1, waiting for transfers between devices, on_device(): lax.psum_scatter(x_part.astype(BF16), 'mp', scatter_dimension=0, tiled=True)  30.5 us
    all_gather x1, blocking collectives, on_device(): back_all = lax.all_gather(back, 'mp', axis=0, tiled=True)  25.4 us
    all_gather x1, blocking collectives, on_device(): x_all = lax.all_gather(x_here[None], 'dp', axis=0, tiled=True)  24.4 us
    unnamed x11, local copies, waits for them, and re-layouts  18.4 us
    reshape x1, local copies, waits for them, and re-layouts, on_device(): weight_grad = weight_grad.reshape(weights.shape)  17.8 us
  transfers between devices with their start and end apart: 3, of which 2 were waited for; matrix products, arithmetic and copies ran while one was open for 23% of the time, Pallas kernels for 4%

profile of v1, /device:TPU:1, one launch (start us, length us, event | category | flops | bytes accessed | tf_op | source)
XLA Modules:
  0.0 370.4 jit_solution(6768193098454925591)
XLA Ops:
  8.1 0.8 fusion.64
  8.9 0.7 compare_select_fusion.4
  10.2 1.9 gather_fusion.1
  12.1 1.9 gather_fusion
  14.0 0.6 fusion.8
  14.6 1.5 fusion.3
  16.2 0.6 pad_maximum_fusion.5
  16.9 13.3 %copy.18 = f32[16,96,2,1536]{3,1,2,0:T(8,128)} copy(bf16[16,96,2,1536]{3,2,1,0:T(2,128)(2,1)} %param.13) | data formatting | bytes 28311552 | tf_op jit(solution)/shard_map/convert_element_type | solution.py:121
  30.3 22.7 %reshape.382 = f32[16,96,2,12,128]{4,3,1,2,0:T(8,128)} reshape(f32[16,96,2,1536]{3,1,2,0:T(8,128)} %copy.18) | data formatting | bytes 37748736 | tf_op jit(solution)/shard_map/convert_element_type | solution.py:121
  53.0 0.2 fusion.18
  53.2 30.5 %reduce-scatter.3.cloned.1.call-done = bf16[96,256]{1,0:T(8,128)(2,1)} async-done(((bf16[1536,256]{1,0:T(8,128)(2,1)}), bf16[96,256]{1,0:T(8,128)(2,1)}) %reduce-scatter.3.cloned.1.call-update) | async-done | bytes 49168 | tf_op jit(solution)/shard_map/reduce_scatter | solution.py:136
  83.8 24.4 %all-gather = bf16[768,256]{1,0:T(8,128)(2,1)S(1)} all-gather(bf16[96,256]{1,0:T(8,128)(2,1)} %reduce-scatter.3.cloned.1.call-done), channel_id=2, replica_groups=mesh['dp'=8,'mp'=16] {'dp'}, dimensions={0}, use_global_device_ids=true | all-gather | bytes 442368 | tf_op jit(solution)/shard_map/all_gather | solution.py:137
  108.2 0.8 fusion.61
  109.0 1.0 fusion.62
  110.0 0.1 fusion.38
  110.1 115.2 %all-gather.3.cloned.1.call-done = bf16[2048,1536]{1,0:T(8,128)(2,1)} async-done(((bf16[16,1536]{1,0:T(8,128)(2,1)}), bf16[2048,1536]{1,0:T(8,128)(2,1)}) %all-gather.3.cloned.1.call-update) | async-done | bytes 6291472 | tf_op jit(solution)/shard_map/all_gather | solution.py:115
  225.3 1.5 convolution_multiply_fusion
  226.8 0.2 reshape.381
  227.1 11.5 %fusion.1 = (f32[16]{0:T(128)S(1)}, bf16[96,12,2,128]{3,1,0,2:T(8,128)(2,1)S(1)}) fusion(f32[16,96,2,12,128]{4,3,1,2,0:T(8,128)} %reshape.382, f32[96,12,2,128]{3,1,0,2:T(8,128)S(1)} %bitcast.44, f32[16]{0:T(128)S(1)} %dynamic-slice_bitcast_fusion), kind=kLoop, calls=%fused_computation.5 | loop fusion | flops 18579440 | bytes 20643968 | tf_op jit(solution)/shard_map/reduce_sum | solution.py:150
  238.6 1.6 fusion.5
  240.2 0.1 fusion.59
  240.3 1.3 convolution_convert_fusion
  241.7 0.1 fusion.36
  241.8 25.4 %all_gather.11.back_ref = bf16[1536,256]{1,0:T(8,128)(2,1)S(1)} all-gather(bf16[96,256]{1,0:T(8,128)(2,1)S(1)} %fusion.36), channel_id=1, replica_groups=mesh['dp'=8,'mp'=16] {'mp'}, dimensions={0}, use_global_device_ids=true | all-gather | bytes 835584 | tf_op jit(solution)/shard_map/all_gather | solution.py:146
  267.2 14.4 %shard_map.111 = (bf16[16,2304,128]{2,1,0:T(8,128)(2,1)}, bf16[256,3072]{1,0:T(8,128)(2,1)}) custom-call(f32[8,16]{1,0:T(8,128)S(1)} %copy-done, bf16[8,96,256]{2,1,0:T(8,128)(2,1)S(1)} %bitcast.41, bf16[8,256,1536]{2,1,0:T(8,128)(2,1)} %bitcast.49, bf16[1536,256]{1,0:T(8,128)(2,1)S(1)} %all_gather.11.back_ref, ...), custom_call_target="tpu_custom_call" | custom-call | flops 10000000000 | bytes 20000000 | tf_op jit(solution)/shard_map/pallas_call | solution.py:76
  281.6 10.6 %copy.33 = bf16[16,96,12,2,128]{4,2,1,3,0:T(8,128)(2,1)} copy(bf16[16,96,12,2,128]{4,3,2,1,0:T(2,128)(2,1)} %bitcast.43) | data formatting | bytes 18874368 | tf_op jit(solution)/shard_map/reshape | solution.py:154
  292.2 17.8 %reshape.380 = bf16[16,96,2,1536]{3,1,2,0:T(8,128)(2,1)} reshape(bf16[16,96,2,12,128]{4,3,1,2,0:T(8,128)(2,1)} %bitcast.42) | data formatting | bytes 18874368 | tf_op jit(solution)/shard_map/reshape | solution.py:155
  310.0 18.4 %copy.20 = bf16[16,96,2,1536]{3,2,1,0:T(2,128)(2,1)} copy(bf16[16,96,2,1536]{3,1,2,0:T(8,128)(2,1)} %reshape.380) | data formatting | bytes 18874368
  328.4 32.6 %psum.7 = f32[16]{0:T(128)S(1)} all-reduce(f32[16]{0:T(128)S(1)} %get-tuple-element.12), channel_id=1, replica_groups=mesh['dp'=8,'mp'=16] {'mp'}, use_global_device_ids=true, to_apply=%region_4.5 | all-reduce | flops 16 | bytes 128 | tf_op jit(solution)/shard_map/psum | solution.py:151
  361.1 0.5 multiply_bitcast_fusion
  361.6 0.8 fusion.60
  362.4 0.6 pad_maximum_fusion.4
  (27 shorter events, 0.4 us)
Async XLA Ops:
  8.0 6.0 %copy-start.2 = (bf16[256,3072]{1,0:T(8,128)(2,1)S(1)}, bf16[256,3072]{1,0:T(8,128)(2,1)}, u32[]{:S(2)}) copy-start(bf16[256,3072]{1,0:T(8,128)(2,1)} %param.8) | copy-start | bytes 4718596
  8.0 6.0 %copy-start.4 = (s32[256]{0:T(256)S(1)}, s32[256]{0:T(256)}, u32[]{:S(2)}) copy-start(s32[256]{0:T(256)} %param.9) | copy-start | bytes 3076
  8.0 75.8 %reduce-scatter.3.cloned.1.call-start = ((), (), s32[]{:S(2)}) async-start(), calls=%async_computation.2 | async-start | bytes 835584 | tf_op jit(solution)/shard_map/reduce_scatter | solution.py:136
  14.6 1.6 copy-start.3
  16.2 209.2 %all-gather.3.cloned.1.call-start = ((), (), s32[]{:S(2)}) async-start(), calls=%async_computation.4 | async-start | bytes 6340608 | tf_op jit(solution)/shard_map/all_gather | solution.py:115
  16.9 344.7 %reduce-scatter.5.cloned.1.call-start = ((), (), s32[]{:S(2)}) async-start(), calls=%async_computation.3 | async-start | bytes 835584 | tf_op jit(solution)/shard_map/reduce_scatter | solution.py:141
  30.3 22.7 %copy-start = (f32[8,16]{1,0:T(8,128)S(1)}, f32[8,16]{1,0:T(8,128)}, u32[]{:S(2)}) copy-start(f32[8,16]{1,0:T(8,128)} %coefs_ref.1) | copy-start | bytes 1540
  238.6 1.8 copy-start.1
Sparse Core Ops, SparseCore 0:
  16.3 67.4 reduce-scatter.2
  241.8 62.7 reduce-scatter.4
Sparse Core Ops, SparseCore 1:
  18.9 206.3 all-gather.2

commit v2 on v1

v2 whole, which is shorter than its diff:
```python
import functools

import jax
import jax.numpy as jnp
from jax import lax
from jax.experimental import pallas as pl
from jax.experimental.pallas import tpu as pltpu
from jax.sharding import PartitionSpec as P

BF16, F32 = jnp.bfloat16, jnp.float32
LANES = 128
MESH = pl.DeviceIdType.MESH
DP, MP = 8, 16
SLICES, COLS = 6, 256
ORDERS = (("z", "y", "x"), ("x", "z", "y"), ("y", "x", "z"))


def dot(a, b, contract):
    return lax.dot_general(a, b, (contract, ((), ())), preferred_element_type=F32)


def turn(rows):
    n = rows.shape[1]
    col = lax.broadcasted_iota(jnp.int32, rows.shape, 1)
    return jnp.where(col // 8 % 2 == 0, pltpu.roll(rows, n - 8, 1), -pltpu.roll(rows, 8, 1))


def interleave(wide, even, odd):
    n = even.shape[0]
    for h in range(2):
        wide[h, pl.ds(0, n, stride=2), :] = even[:, h * LANES : (h + 1) * LANES]
        wide[h, pl.ds(1, n, stride=2), :] = odd[:, h * LANES : (h + 1) * LANES]
    return jnp.concatenate([wide[0], wide[1]], 1)


def separate(wide, both):
    n = both.shape[0] // 2
    for h in range(2):
        wide[h] = both[:, h * LANES : (h + 1) * LANES]
    return [
        jnp.concatenate([wide[h, pl.ds(part, n, stride=2), :] for h in range(2)], 1) for part in range(2)
    ]


def remote(src, dst, send, recv, target):
    return pltpu.make_async_remote_copy(
        src_ref=src, dst_ref=dst, send_sem=send, recv_sem=recv, device_id=target, device_id_type=MESH
    )


def column_of(row):
    n = row.shape[1]
    same = lax.broadcasted_iota(jnp.int32, (n, n), 0) == lax.broadcasted_iota(jnp.int32, (n, n), 1)
    return jnp.sum(jnp.where(same, row, 0.0), 1, keepdims=True)


def exchange_kernel(
    scale, norm,
    feats_hbm, targets_ref, rolls_ref, counts_ref, coefs_ref, weights_hbm, angles_ref, cot_ref,
    atom_ref, coef_ref, spread_ref, x_hbm, back_hbm, cot_hbm,
    feats, weights, merged, mine, crystal, cots, x_parts, x_slots, x_all, back_all, out_parts, out_slots,
    coef_parts, wide,
    load_sem, weight_sem, store_sem,
    cry_s, cry_r, x_s, x_r, xd_s, xd_r, back_s, back_r, out_s, out_r, coef_s, coef_r,
    swap_s, swap_r, ring_s, ring_r, fin_s, fin_r,
):
    d, m = lax.axis_index("dp"), lax.axis_index("mp")
    z, y, x, core = d // 2, m // 8 * 2 + d % 2, m // 2 % 4, m % 2
    experts, rows = weights.shape[1], weights.shape[2]
    width = crystal.shape[2]
    tiles = width // LANES
    other = 1 - core
    sibling = (d, m + 1 - 2 * core)

    def device(z, y, x):
        return (z * 2 + y % 2, y // 2 * 8 + x * 2 + core)

    def mp_peer(j):
        return (d, lax.rem(m + j, MP))

    def dp_peer(j):
        return (lax.rem(d + j, DP), m)

    def each(n, body):
        lax.fori_loop(1, n, lambda j, c: (body(j), c)[1], 0)

    def span(start, stop, body):
        lax.fori_loop(start, stop, lambda j, c: (body(j), c)[1], 0)

    barrier = pltpu.get_barrier_semaphore()
    each(MP, lambda j: pl.semaphore_signal(barrier, inc=1, device_id=mp_peer(j), device_id_type=MESH))
    each(DP, lambda j: pl.semaphore_signal(barrier, inc=1, device_id=dp_peer(j), device_id_type=MESH))
    across = (d + 1 - 2 * (d % 2), lax.rem(m + 8, MP))
    pl.semaphore_signal(barrier, inc=1, device_id=across, device_id_type=MESH)

    feats_copy = pltpu.make_async_copy(feats_hbm, feats, load_sem)
    feats_copy.start()

    def weight_copy(t):
        return pltpu.make_async_copy(
            weights_hbm.at[:, :, :, pl.ds(pl.multiple_of(t * LANES, LANES), LANES)], weights.at[t], weight_sem.at[t]
        )

    span(0, tiles, lambda t: weight_copy(t).start())

    c = cot_ref[...].astype(F32)
    own = jnp.concatenate([c[:, :width], c[:, width:]], 0).astype(BF16)
    crystal[m] = own
    for s in range(SLICES):
        mine[s] = own[:, s * COLS : (s + 1) * COLS]
    for o in range(3):
        cots[3 * core + o, z, y, x, core] = mine[3 * core + o]

    slots = targets_ref.shape[1]
    table = rolls_ref[...] == lax.broadcasted_iota(jnp.int32, (angles_ref.shape[1], slots), 0)
    angle = column_of(angles_ref[...])
    valid = lax.broadcasted_iota(jnp.int32, (1, slots), 1) < counts_ref[0]
    factor = jnp.where(valid, scale, 0.0)
    cosine = column_of(jnp.sum(jnp.where(table, jnp.cos(angle), 0.0), 0, keepdims=True) * factor)
    sine = column_of(jnp.sum(jnp.where(table, jnp.sin(angle), 0.0), 0, keepdims=True) * factor)
    target = column_of(targets_ref[...].astype(F32)).astype(jnp.int32)
    q = lax.broadcasted_iota(jnp.int32, (slots, spread_ref.shape[2]), 1)
    hit = target == q // 16 * 8 + q % 8
    real = q // 8 % 2 == 0
    spread_ref[0] = jnp.where(hit, jnp.where(real, cosine, sine), 0.0).astype(BF16)
    spread_ref[1] = jnp.where(hit, jnp.where(real, -sine, cosine), 0.0).astype(BF16)

    pl.semaphore_wait(barrier, MP - 1 + DP - 1 + 1)

    swap = remote(
        mine.at[pl.ds(3 * other, 3)], cots.at[pl.ds(3 * other, 3), z, y, x, core], swap_s, swap_r, sibling
    )
    swap.start()
    each(MP, lambda j: remote(crystal.at[m], crystal.at[m], cry_s.at[j - 1], cry_r.at[j - 1], mp_peer(j)).start())

    here = {"z": z, "y": y, "x": x}

    def region(o, stage, value, half=None):
        order = ORDERS[o]
        index = dict(here)
        for a in order[:stage]:
            index[a] = slice(None)
        index[order[stage]] = value
        at = (3 * core + o, index["z"], index["y"], index["x"])
        return cots.at[at if half is None else at + (half,)]

    def neighbour(o, stage, by):
        to = dict(here)
        a = ORDERS[o][stage]
        to[a] = (here[a] + by) % 4
        return device(to["z"], to["y"], to["x"])

    def ring_copy(o, stage, kind):
        a = here[ORDERS[o][stage]]
        by = 1 if kind % 2 == 0 else 3
        value = a if kind < 2 else (a + 3) % 4 if kind == 2 else (a + 1) % 4
        ref = region(o, stage, value, None if kind < 2 else kind - 2)
        sem = (o * 3 + stage) * 4 + kind
        return remote(ref, ref, ring_s.at[sem], ring_r.at[sem], neighbour(o, stage, by))

    def ring_arrival(o, stage, kind):
        a = here[ORDERS[o][stage]]
        value = (a + 3) % 4 if kind == 0 else (a + 1) % 4 if kind == 1 else (a + 2) % 4
        ref = region(o, stage, value, None if kind < 2 else kind - 2)
        sem = (o * 3 + stage) * 4 + kind
        return remote(ref, ref, ring_s.at[sem], ring_r.at[sem], neighbour(o, stage, 1))

    def ring_first(stage):
        for o in range(3):
            for kind in (0, 1):
                ring_copy(o, stage, kind).start()

    def ring_second(stage):
        for o in range(3):
            for kind in (0, 1):
                ring_arrival(o, stage, kind).wait_recv()
                ring_copy(o, stage, kind + 2).start()

    def ring_end(stage):
        for o in range(3):
            for kind in (2, 3):
                ring_arrival(o, stage, kind).wait_recv()

    feats_copy.wait()
    group = 4
    block = group * rows

    def spread_block(i):
        plus = feats[:, pl.ds(pl.multiple_of(i * block, block), block)]
        minus = feats[:, pl.ds(pl.multiple_of(width + i * block, block), block)]
        part = dot(plus, spread_ref[0], ((0,), (0,))) + dot(minus, spread_ref[1], ((0,), (0,)))
        x_parts[pl.ds(i * group, group)] = part.astype(BF16).reshape(group, rows, -1)

    span(0, width // block, spread_block)

    def x_copy(j):
        return remote(
            x_parts.at[lax.rem(m + j, MP)], x_slots.at[j - 1], x_s.at[j - 1], x_r.at[j - 1], mp_peer(j)
        )

    each(MP, lambda j: x_copy(j).start())
    swap.wait_recv()
    ring_first(0)

    def merge(t):
        weight_copy(t).wait()
        total = jnp.zeros((2 * rows, LANES), F32)
        for k in range(experts):
            total += coefs_ref[d, k] * weights[t, k].reshape(2 * rows, LANES).astype(F32)
        merged[:, pl.ds(pl.multiple_of(t * LANES, LANES), LANES)] = total.astype(BF16)

    span(0, tiles // 3, merge)
    ring_second(0)
    span(tiles // 3, 2 * tiles // 3, merge)
    ring_end(0)
    ring_first(1)
    span(2 * tiles // 3, tiles, merge)

    def cry_copy(j):
        return remote(crystal.at[m], crystal.at[m], cry_s.at[j - 1], cry_r.at[j - 1], mp_peer(j))

    def cry_arrival(j):
        at = crystal.at[lax.rem(m - j + MP, MP)]
        return remote(at, at, cry_s.at[j - 1], cry_r.at[j - 1], mp_peer(j))

    each(MP, lambda j: cry_arrival(j).wait_recv())
    cot_rows = crystal[...].reshape(-1, width)
    by_real, by_imag = separate(wide, dot(merged[...], cot_rows, ((1,), (1,))))
    back_all[m] = (by_real + turn(by_imag)).astype(BF16)

    def back_copy(j):
        return remote(back_all.at[m], back_all.at[m], back_s.at[j - 1], back_r.at[j - 1], mp_peer(j))

    def back_arrival(j):
        at = back_all.at[lax.rem(m - j + MP, MP)]
        return remote(at, at, back_s.at[j - 1], back_r.at[j - 1], mp_peer(j))

    each(MP, lambda j: back_copy(j).start())
    ring_second(1)

    def x_add(j, total):
        x_copy(j).wait_recv()
        return total + x_slots[j - 1].astype(F32)

    x_here = lax.fori_loop(1, MP, x_add, x_parts[m].astype(F32)).astype(BF16)
    x_all[d] = x_here

    def xd_copy(j):
        return remote(x_all.at[d], x_all.at[d], xd_s.at[j - 1], xd_r.at[j - 1], dp_peer(j))

    def xd_arrival(j):
        at = x_all.at[lax.rem(d - j + DP, DP)]
        return remote(at, at, xd_s.at[j - 1], xd_r.at[j - 1], dp_peer(j))

    each(DP, lambda j: xd_copy(j).start())
    x_wide = x_here.astype(F32)
    both = interleave(wide, x_wide, -turn(x_wide)).astype(BF16)

    def out_block(i):
        cols = pl.ds(pl.multiple_of(i * block, block), block)
        sent = dot(both, merged[:, cols], ((0,), (0,))).astype(BF16)
        out_parts[:, :, cols] = sent.reshape(MP, 16, block)

    span(0, width // block, out_block)

    def out_copy(j):
        return remote(
            out_parts.at[lax.rem(m + j, MP)], out_slots.at[j - 1], out_s.at[j - 1], out_r.at[j - 1], mp_peer(j)
        )

    each(MP, lambda j: out_copy(j).start())
    ring_end(1)
    ring_first(2)

    def coef_add(t, sums):
        cols = pl.ds(pl.multiple_of(t * LANES, LANES), LANES)
        grad = dot(both, crystal[:, :, cols].reshape(-1, LANES), ((1,), (0,))) * norm
        added = []
        for k in range(experts):
            terms = weights[t, k].reshape(2 * rows, LANES).astype(F32) * grad
            added.append(sums[k] + jnp.sum(terms.reshape(-1, 8, LANES), 0))
        return tuple(added)

    sums = tuple(jnp.zeros((8, LANES), F32) for _ in range(experts))
    sums = lax.fori_loop(0, tiles // 2, coef_add, sums)
    ring_second(2)
    sums = lax.fori_loop(tiles // 2, tiles, coef_add, sums)
    coef_parts[0] = jnp.concatenate([jnp.sum(v, 0, keepdims=True) for v in sums], 0)

    def coef_copy(j):
        return remote(coef_parts.at[0], coef_parts.at[j], coef_s.at[j - 1], coef_r.at[j - 1], mp_peer(j))

    each(MP, lambda j: coef_copy(j).start())

    ring_end(2)

    def fin_copy(o):
        at = cots.at[3 * core + o]
        return remote(at, at, fin_s.at[o], fin_r.at[o], sibling)

    def fin_arrival(o):
        at = cots.at[3 * other + o]
        return remote(at, at, fin_s.at[o], fin_r.at[o], sibling)

    def cot_store(s, n):
        return pltpu.make_async_copy(cots.at[s], cot_hbm.at[s], store_sem.at[n])

    for o in range(3):
        fin_copy(o).start()
        cot_store(3 * core + o, o).start()

    each(MP, lambda j: back_arrival(j).wait_recv())
    back_store = pltpu.make_async_copy(back_all, back_hbm, store_sem.at[6])
    back_store.start()
    each(DP, lambda j: xd_arrival(j).wait_recv())
    x_store = pltpu.make_async_copy(x_all, x_hbm, store_sem.at[7])
    x_store.start()

    def out_add(j, out):
        out_copy(j).wait_recv()
        return out + out_slots[j - 1].astype(F32)

    out = lax.fori_loop(1, MP, out_add, out_parts[m].astype(F32))
    atom_ref[...] = jnp.concatenate([out[:8], out[8:]], 1).astype(BF16)

    each(MP, lambda j: coef_copy(j).wait_recv())
    lanes = jnp.sum(jnp.sum(coef_parts[...], 0), 1, keepdims=True) * (width**-0.5)
    same = lax.broadcasted_iota(jnp.int32, (experts, experts), 0) == lax.broadcasted_iota(
        jnp.int32, (experts, experts), 1
    )
    coef_ref[...] = jnp.sum(jnp.where(same, lanes, 0.0), 0, keepdims=True)

    for o in range(3):
        fin_arrival(o).wait_recv()
        cot_store(3 * other + o, 3 + o).start()

    swap.wait_send()
    each(MP, lambda j: cry_copy(j).wait_send())
    each(MP, lambda j: x_copy(j).wait_send())
    each(MP, lambda j: back_copy(j).wait_send())
    each(DP, lambda j: xd_copy(j).wait_send())
    each(MP, lambda j: out_copy(j).wait_send())
    each(MP, lambda j: coef_copy(j).wait_send())
    for o in range(3):
        for stage in range(3):
            for kind in range(4):
                ring_copy(o, stage, kind).wait_send()
        fin_copy(o).wait_send()
        cot_store(3 * core + o, o).wait()
        cot_store(3 * other + o, 3 + o).wait()
    back_store.wait()
    x_store.wait()


def exchange(edge_feats, targets, roll_ids, counts, coefs, weights, roll_angles, atom_cot):
    slots, double = edge_feats.shape
    width = double // 2
    experts, rows = weights.shape[:2]
    atoms_here = atom_cot.shape[0]
    q = 2 * MP * atoms_here
    vmem = pl.BlockSpec(memory_space=pltpu.VMEM)
    smem = pl.BlockSpec(memory_space=pltpu.SMEM)
    hbm = pl.BlockSpec(memory_space=pl.ANY)
    dma = pltpu.SemaphoreType.DMA
    cots = (SLICES, 4, 4, 4, 2, 16, COLS)
    return pl.pallas_call(
        functools.partial(
            exchange_kernel, (atoms_here / slots) ** 0.5, (slots * MP) ** -0.5
        ),
        in_specs=[hbm, vmem, vmem, smem, smem, hbm, vmem, vmem],
        out_specs=[vmem, vmem, vmem, hbm, hbm, hbm],
        out_shape=[
            jax.ShapeDtypeStruct(atom_cot.shape, BF16),
            jax.ShapeDtypeStruct((1, experts), F32),
            jax.ShapeDtypeStruct((2, slots, q), BF16),
            jax.ShapeDtypeStruct((DP, rows, q), BF16),
            jax.ShapeDtypeStruct((MP, rows, q), BF16),
            jax.ShapeDtypeStruct(cots, BF16),
        ],
        scratch_shapes=[
            pltpu.VMEM(edge_feats.shape, BF16),
            pltpu.VMEM((width // LANES, experts, rows, 2, LANES), BF16),
            pltpu.VMEM((2 * rows, width), BF16),
            pltpu.VMEM((SLICES, 16, COLS), BF16),
            pltpu.VMEM((MP, 16, width), BF16),
            pltpu.VMEM(cots, BF16),
            pltpu.VMEM((MP, rows, q), BF16),
            pltpu.VMEM((MP - 1, rows, q), BF16),
            pltpu.VMEM((DP, rows, q), BF16),
            pltpu.VMEM((MP, rows, q), BF16),
            pltpu.VMEM((MP, 16, width), BF16),
            pltpu.VMEM((MP - 1, 16, width), BF16),
            pltpu.VMEM((MP, experts, LANES), F32),
            pltpu.VMEM((2, 2 * rows, LANES), F32),
            dma(()), dma((width // LANES,)), dma((8,)),
        ]
        + [dma((n - 1,)) for n in (MP, MP, DP, MP, MP, MP) for _ in range(2)]
        + [dma(()), dma(()), dma((36,)), dma((36,)), dma((3,)), dma((3,))],
        compiler_params=pltpu.CompilerParams(
            collective_id=0, has_side_effects=True, vmem_limit_bytes=56 * 2**20
        ),
        cost_estimate=pl.CostEstimate(flops=4 * 10**9, bytes_accessed=2 * 10**7, transcendentals=0),
    )(
        edge_feats, targets[None], roll_ids[None], counts, coefs, weights, roll_angles[None], atom_cot
    )


def mix_kernel(norm, coefs_ref, x_ref, cot_ref, back_ref, spread_ref, wg_hbm, eg_ref, both_ref, wide, gm_ref, left_ref,
               out_ref, sem):
    step, steps = pl.program_id(0), pl.num_programs(0)
    crystals, rows, _ = x_ref.shape
    experts = wg_hbm.shape[0]

    @pl.when(step == 0)
    def _():
        r = lax.broadcasted_iota(jnp.int32, (16 * experts, 16 * crystals), 0)
        c = lax.broadcasted_iota(jnp.int32, (16 * experts, 16 * crystals), 1)
        pieces = []
        for k in range(experts):
            row = jnp.zeros((16, 16 * crystals), F32)
            for i in range(crystals):
                row = jnp.where(c[:16] // 16 == i, coefs_ref[i, k], row)
            pieces.append(row)
        mixed = jnp.where(r % 16 == c % 16, jnp.concatenate(pieces, 0), 0.0)
        high = mixed.astype(BF16)
        left_ref[:, : 16 * crystals] = high
        left_ref[:, 16 * crystals :] = (mixed - high.astype(F32)).astype(BF16)
        for i in range(crystals):
            x = x_ref[i].astype(F32)
            both_ref[i] = interleave(wide, x, -turn(x)).astype(BF16)

    for i in range(crystals):
        cot = jnp.concatenate(
            [cot_ref[0, i // 2, i % 2 + 2 * h].reshape(LANES, COLS) for h in range(2)], 0
        )
        gm_ref[i] = (dot(both_ref[i], cot, ((1,), (0,))) * norm).astype(BF16)

    slot = lax.rem(step, 2)

    def copies(step):
        slot = lax.rem(step, 2)
        return [
            pltpu.make_async_copy(
                out_ref.at[slot, t],
                wg_hbm.at[:, :, :, pl.ds(pl.multiple_of(step * COLS + t * LANES, LANES), LANES)],
                sem.at[slot, t],
            )
            for t in range(2)
        ]

    @pl.when(step >= 2)
    def _():
        for copy in copies(step - 2):
            copy.wait()

    for g in range(2 * rows // 16):
        right = jnp.concatenate([gm_ref[i, g * 16 : (g + 1) * 16, :] for i in range(crystals)] * 2, 0)
        out = dot(left_ref[...], right, ((1,), (0,))).astype(BF16)
        for t in range(2):
            for k in range(experts):
                piece = out[k * 16 : (k + 1) * 16, t * LANES : (t + 1) * LANES]
                out_ref[slot, t, k, g * 8 : (g + 1) * 8] = piece.reshape(8, 2, LANES)

    for copy in copies(step):
        copy.start()

    part = step // (steps // 2)
    cols = eg_ref.shape[1]
    at = pl.multiple_of(step % (steps // 2) * cols, cols)
    eg_ref[...] = dot(spread_ref[part], back_ref[pl.ds(at, cols), :], ((1,), (1,))).astype(BF16)

    @pl.when(step == steps - 1)
    def _():
        for copy in copies(step - 1) + copies(step):
            copy.wait()


def mix(coefs, x_all, cot_all, back_all, spread, norm):
    crystals, experts = coefs.shape
    _, rows, q = x_all.shape
    width = back_all.shape[0]
    slots = spread.shape[1]
    whole = lambda shape: pl.BlockSpec(shape, lambda i: (0,) * len(shape))
    return pl.pallas_call(
        functools.partial(mix_kernel, norm),
        grid=(SLICES,),
        in_specs=[
            pl.BlockSpec(memory_space=pltpu.SMEM),
            whole(x_all.shape),
            pl.BlockSpec((1,) + cot_all.shape[1:], lambda i: (i,) + (0,) * 6),
            whole(back_all.shape),
            whole(spread.shape),
        ],
        out_specs=[
            pl.BlockSpec(memory_space=pl.ANY),
            pl.BlockSpec((slots, 2 * width // SLICES), lambda i: (0, i)),
        ],
        out_shape=[
            jax.ShapeDtypeStruct((experts, rows, 2, width), BF16),
            jax.ShapeDtypeStruct((slots, 2 * width), BF16),
        ],
        scratch_shapes=[
            pltpu.VMEM((crystals, 2 * rows, q), BF16),
            pltpu.VMEM((2, 2 * rows, LANES), F32),
            pltpu.VMEM((crystals, 2 * rows, COLS), BF16),
            pltpu.VMEM((16 * experts, 32 * crystals), BF16),
            pltpu.VMEM((2, 2, experts, rows, 2, LANES), BF16),
            pltpu.SemaphoreType.DMA((2, 2)),
        ],
        compiler_params=pltpu.CompilerParams(vmem_limit_bytes=40 * 2**20),
        cost_estimate=pl.CostEstimate(flops=10**10, bytes_accessed=2 * 10**7, transcendentals=0),
    )(coefs, x_all, cot_all, back_all, spread)


def on_device(edge_feats, targets, roll_ids, counts, coefs, weights, roll_angles, atom_cot):
    slots = edge_feats.shape[0]
    atom_out, coef_grad, spread, x_all, back_all, cot_all = exchange(
        edge_feats, targets, roll_ids, counts, coefs, weights, roll_angles, atom_cot
    )
    back_all = back_all.reshape(-1, back_all.shape[2])
    weight_grad, edge_grad = mix(coefs, x_all, cot_all, back_all, spread, (slots * MP) ** -0.5)
    return (atom_out, edge_grad, weight_grad, coef_grad)


def solution(mesh):
    placed = (
        P(("dp", "mp"), None),
        P(("dp", "mp")),
        P(("dp", "mp")),
        P(("dp", "mp")),
        P(),
        P(None, "mp", None, None),
        P(),
        P(("dp", "mp"), None),
    )
    return jax.shard_map(
        on_device,
        mesh=mesh,
        in_specs=placed,
        out_specs=(
            P(("dp", "mp"), None),
            P(("dp", "mp"), None),
            P(None, "mp", None, None),
            P("dp", None),
        ),
        check_vma=False,
    )
```

time: 372 us -> 101 us (0.27)
  waiting for transfers between devices: 146 us -> 0 us
  local copies, waits for them, and re-layouts: 90.4 us -> 7 us
  blocking collectives: 82.5 us -> 0 us
  Pallas kernels: 14.4 us -> 92.4 us
  between operations: 16.3 us -> 1.33 us
  other arithmetic: 14.5 us -> 0 us
  matrix products: 6.46 us -> 0 us
    all_gather x1 -> x0, waiting for transfers between devices: 115 us -> none  [on_device(): lax.all_gather(cot_rows, ('dp', 'mp'), axis=0, tiled=True)]
    pallas_call x1 -> x2, Pallas kernels: 14.4 us -> 92.4 us  [the longest x1 79.3 us: exchange(): pl.pallas_call(functools.partial(exchange_kernel, (atoms_here / slots) **...]
    all_gather x2 -> x0, blocking collectives: 49.8 us -> none  [the longest x1 25.4 us: on_device(): back_all = lax.all_gather(back, 'mp', axis=0, tiled=True)]
    convert_element_type x2 -> x0, local copies, waits for them, and re-layouts: 36 us -> none  [on_device(): merged = jnp.sum(coef_row[:, None, None] * flat.astype(F32), 0).astype(BF16)]
    psum x1 -> x0, blocking collectives: 32.6 us -> none  [on_device(): coef_grad = (lax.psum(local_coef, 'mp') / width ** 0.5)[None, :]]
    reduce_scatter x2 -> x0, waiting for transfers between devices: 30.5 us -> none  [the longest x1 30.5 us: on_device(): lax.psum_scatter(x_part.astype(BF16), 'mp', scatter_dimension=0, tiled=True)]
    reshape x3 -> x0, local copies, waits for them, and re-layouts: 28.7 us -> none  [the longest x1 17.8 us: on_device(): weight_grad = weight_grad.reshape(weights.shape)]
    reduce_sum x1 -> x0, other arithmetic: 11.5 us -> none  [on_device(): local_coef = jnp.sum(flat.astype(F32) * grad_flat[None], (1, 2))]
  transfers between devices with their start and end apart: 3 -> 0, of which waited for: 2 -> 0; matrix products, arithmetic and copies ran while one was open for 23% -> 0% of each run, Pallas kernels for 4% -> 0%
where the time goes in v2:
time: 101 us
  Pallas kernels  92.4 us (91%)
  local copies, waits for them, and re-layouts  7 us (7%)
  between operations  1.33 us (1%)
    pallas_call x1, Pallas kernels, exchange(): pl.pallas_call(functools.partial(exchange_kernel, (atoms_here / slots) **...  79.3 us
    pallas_call x1, Pallas kernels, mix(): pl.pallas_call(functools.partial(mix_kernel, norm), grid=(SLICES,), in_sp...  13 us
    unnamed x16, local copies, waits for them, and re-layouts  7 us

profile of v2, /device:TPU:1, one launch (start us, length us, event | category | flops | bytes accessed | tf_op | source)
XLA Modules:
  0.0 100.7 jit_solution(2583580152282477266)
XLA Ops:
  1.3 0.0 copy-start
  1.3 79.3 %shard_map.111 = (bf16[8,3072]{1,0:T(8,128)(2,1)}, f32[1,16]{1,0:T(1,128)}, bf16[2,256,256]{2,1,0:T(8,128)(2,1)}, bf16[8,96,256]{2,1,0:T(8,128)(2,1)}, bf16[16,9...) custom-call(bf16[256,3072]{1,0:T(8,128)(2,1)} %feats_hbm.1, s32[1,256]{1,0:T(1,128)} %bitcast.5, ...), custom_call_target="tpu_custom_call" | custom-call | flops 4000000000 | bytes 20000000 | tf_op jit(solution)/shard_map/pallas_call | solution.py:366
  80.6 0.0 copy-done
  80.6 0.0 copy-start.1
  80.6 1.1 %copy-done.1 = bf16[16,96,256]{2,1,0:T(8,128)(2,1)S(1)} copy-done((bf16[16,96,256]{2,1,0:T(8,128)(2,1)S(1)}, bf16[16,96,256]{2,1,0:T(8,128)(2,1)}, u32[]{:S(2)}) %copy-start.1) | copy-done | bytes 786456
  81.8 0.0 copy-start.2
  81.8 2.8 %copy-done.2 = bf16[6,4,4,4,2,16,256]{6,5,4,3,2,1,0:T(8,128)(2,1)S(1)} copy-done((bf16[6,4,4,4,2,16,256]{6,5,4,3,2,1,0:T(8,128)(2,1)S(1)}, bf16[6,4,4,4,2,16,256]{6,5,4,3,2,1,0:T(8,128)(2,1)}, u32[]{:S(2)}) %copy-start.2) | copy-done | bytes 6291480
  84.5 0.0 copy-start.3
  84.5 1.0 copy-done.3
  85.5 0.0 copy-start.4
  85.5 0.9 copy-done.4
  86.5 0.0 copy-start.5
  86.5 0.0 copy-start.6
  86.5 13.0 %shard_map.112 = (bf16[16,96,2,1536]{3,2,1,0:T(2,128)(2,1)}, bf16[256,3072]{1,0:T(8,128)(2,1)}) custom-call(f32[8,16]{1,0:T(8,128)S(1)} %copy-done, bf16[8,96,256]{2,1,0:T(8,128)(2,1)S(1)} %copy-done.3, bf16[6,4,4,4,2,16,256]{6,5,4,3,2,1,0:T(8,128)(2,1)S(1)} %copy-done.2, bf16[1536,256]{1,0:T(8,128)(2,1)S(1)} %bitcast.4, bf16[2,256,256]{2,1,0:T(8,128)(2,1)S(1)} %copy-done.4), custom_call_target="tpu_custom_call" | custom-call | flops 10000000000 | bytes 20000000 | tf_op jit(solution)/shard_map/pallas_call | solution.py:484
  99.5 0.0 copy-done.5
  99.5 0.6 copy.15
  100.2 0.0 copy-done.6
  100.2 0.5 copy.16
Async XLA Ops:
  1.3 79.3 %copy-start = (f32[8,16]{1,0:T(8,128)S(1)}, f32[8,16]{1,0:T(8,128)}, u32[]{:S(2)}) copy-start(f32[8,16]{1,0:T(8,128)} %coefs_ref.3) | copy-start | bytes 1540
  80.6 1.1 %copy-start.1 = (bf16[16,96,256]{2,1,0:T(8,128)(2,1)S(1)}, bf16[16,96,256]{2,1,0:T(8,128)(2,1)}, u32[]{:S(2)}) copy-start(bf16[16,96,256]{2,1,0:T(8,128)(2,1)} %get-tuple-element.15) | copy-start | bytes 2359300
  81.8 2.8 %copy-start.2 = (bf16[6,4,4,4,2,16,256]{6,5,4,3,2,1,0:T(8,128)(2,1)S(1)}, bf16[6,4,4,4,2,16,256]{6,5,4,3,2,1,0:T(8,128)(2,1)}, u32[]{:S(2)}) copy-start(bf16[6,4,4,4,2,16,256]{6,5,4,3,2,1,0:T(8,128)(2,1)} %get-tuple-element.14.cot_ref) | copy-start | bytes 18874372
  84.5 1.0 copy-start.3
  85.5 0.9 copy-start.4
  86.5 13.1 %copy-start.5 = (bf16[8,3072]{1,0:T(8,128)(2,1)S(1)}, bf16[8,3072]{1,0:T(8,128)(2,1)}, u32[]{:S(2)}) copy-start(bf16[8,3072]{1,0:T(8,128)(2,1)} %get-tuple-element.24) | copy-start | bytes 147460
  86.5 13.7 %copy-start.6 = (f32[1,16]{1,0:T(1,128)S(1)}, f32[1,16]{1,0:T(1,128)}, u32[]{:S(2)}) copy-start(f32[1,16]{1,0:T(1,128)} %get-tuple-element.27) | copy-start | bytes 196

commit v3 on v2

v3 whole, which is shorter than its diff:
```python
import functools

import jax
import jax.numpy as jnp
from jax import lax
from jax.experimental import pallas as pl
from jax.experimental.pallas import tpu as pltpu
from jax.sharding import PartitionSpec as P

BF16, F32 = jnp.bfloat16, jnp.float32
LANES = 128
MESH = pl.DeviceIdType.MESH
DP, MP = 8, 16
SLICES, COLS = 6, 256
ORDERS = (("x", "y", "z"), ("y", "x", "z"), ("z", "x", "y"))
SWAP, RING, PLANE, X_SUM, OUT_SUM, BACK, X_DP, COEF = 0, 1, 37, 49, 55, 61, 70, 75
COPIES = COEF + MP - 1


def dot(a, b, contract):
    return lax.dot_general(a, b, (contract, ((), ())), preferred_element_type=F32)


def turn(rows):
    n = rows.shape[1]
    col = lax.broadcasted_iota(jnp.int32, rows.shape, 1)
    return jnp.where(col // 8 % 2 == 0, pltpu.roll(rows, n - 8, 1), -pltpu.roll(rows, 8, 1))


def interleave(wide, even, odd):
    n = even.shape[0]
    for h in range(2):
        wide[h, pl.ds(0, n, stride=2), :] = even[:, h * LANES : (h + 1) * LANES]
        wide[h, pl.ds(1, n, stride=2), :] = odd[:, h * LANES : (h + 1) * LANES]
    return jnp.concatenate([wide[0], wide[1]], 1)


def separate(wide, both):
    n = both.shape[0] // 2
    for h in range(2):
        wide[h] = both[:, h * LANES : (h + 1) * LANES]
    return [
        jnp.concatenate([wide[h, pl.ds(part, n, stride=2), :] for h in range(2)], 1) for part in range(2)
    ]


def remote(src, dst, send, recv, target):
    return pltpu.make_async_remote_copy(
        src_ref=src, dst_ref=dst, send_sem=send, recv_sem=recv, device_id=target, device_id_type=MESH
    )


def column_of(row):
    n = row.shape[1]
    same = lax.broadcasted_iota(jnp.int32, (n, n), 0) == lax.broadcasted_iota(jnp.int32, (n, n), 1)
    return jnp.sum(jnp.where(same, row, 0.0), 1, keepdims=True)


def exchange_kernel(
    scale, norm,
    feats_hbm, targets_ref, rolls_ref, counts_ref, coefs_ref, weights_hbm, angles_ref, cot_ref,
    atom_ref, coef_ref, spread_ref, x_hbm, back_hbm, cot_hbm,
    feats, weights, merged, mine, crystal, cots, x_all, back_all, coef_parts, wide,
    x_parts, x_pair, x_held, x_one, x_two, x_cross, out_parts, out_pair, out_held, out_one, out_two, out_cross,
    load_sem, weight_sem, store_sem, send_sem, recv_sem,
):
    d, m = lax.axis_index("dp"), lax.axis_index("mp")
    z, y, x, core = d // 2, m // 8 * 2 + d % 2, m // 2 % 4, m % 2
    y_hi, y_lo = m // 8, d % 2
    tiles, experts, double, _ = weights.shape
    rows, width = double // 2, tiles * LANES
    other = 1 - core
    ahead, behind, far = (x + 1) % 4, (x + 3) % 4, (x + 2) % 4

    def device(z, y, x, core):
        return (z * 2 + y % 2, y // 2 * 8 + x * 2 + core)

    sibling = device(z, y, x, other)
    x_next, x_last = device(z, y, ahead, core), device(z, y, behind, core)
    y_peer = device(z, (y + 2) % 4, x, core)
    z_next, z_last = device((z + 1) % 4, y, x, core), device((z + 3) % 4, y, x, core)
    y_next, y_last = device(z, (y + 1) % 4, x, core), device(z, (y + 3) % 4, x, core)
    lo_peer = (d + 1 - 2 * y_lo, m)

    def mp_peer(j):
        return (d, lax.rem(m + j, MP))

    def span(start, stop, body):
        lax.fori_loop(start, stop, lambda j, c: (body(j), c)[1], 0)

    barrier = pltpu.get_barrier_semaphore()
    span(1, MP, lambda j: pl.semaphore_signal(barrier, inc=1, device_id=mp_peer(j), device_id_type=MESH))
    for to in (z_next, z_last, y_next, y_last):
        pl.semaphore_signal(barrier, inc=1, device_id=to, device_id_type=MESH)

    feats_copy = pltpu.make_async_copy(feats_hbm, feats, load_sem)
    feats_copy.start()
    weight_rows = weights_hbm.reshape(experts, double, width)

    def weight_copy(t):
        cols = pl.ds(pl.multiple_of(t * LANES, LANES), LANES)
        return pltpu.make_async_copy(weight_rows.at[:, :, cols], weights.at[t], weight_sem.at[t])

    span(0, tiles, lambda t: weight_copy(t).start())

    sent = []

    def send(sem, src, dst, to):
        copy = remote(src, dst, send_sem.at[sem], recv_sem.at[sem], to)
        copy.start()
        sent.append(copy)

    def arrive(sem, ref):
        remote(ref, ref, send_sem.at[sem], recv_sem.at[sem], sibling).wait_recv()

    c = cot_ref[...].astype(F32)
    own = jnp.concatenate([c[:, :width], c[:, width:]], 0).astype(BF16)
    for s in range(SLICES):
        mine[s] = own[:, s * COLS : (s + 1) * COLS]
    for o in range(3):
        cots[3 * core + o, z, y, x, core] = mine[3 * core + o]

    slots = targets_ref.shape[1]
    table = rolls_ref[...] == lax.broadcasted_iota(jnp.int32, (angles_ref.shape[1], slots), 0)
    angle = column_of(angles_ref[...])
    valid = lax.broadcasted_iota(jnp.int32, (1, slots), 1) < counts_ref[0]
    factor = jnp.where(valid, scale, 0.0)
    cosine = column_of(jnp.sum(jnp.where(table, jnp.cos(angle), 0.0), 0, keepdims=True) * factor)
    sine = column_of(jnp.sum(jnp.where(table, jnp.sin(angle), 0.0), 0, keepdims=True) * factor)
    target = column_of(targets_ref[...].astype(F32)).astype(jnp.int32)
    q = lax.broadcasted_iota(jnp.int32, (slots, spread_ref.shape[2]), 1)
    hit = target == q // 16 * 8 + q % 8
    real = q // 8 % 2 == 0
    spread_ref[0] = jnp.where(hit, jnp.where(real, cosine, sine), 0.0).astype(BF16)
    spread_ref[1] = jnp.where(hit, jnp.where(real, -sine, cosine), 0.0).astype(BF16)

    pl.semaphore_wait(barrier, MP - 1 + 4)

    theirs = pl.ds(3 * other, 3)
    send(SWAP, mine.at[theirs], cots.at[theirs, z, y, x, core], sibling)

    here = {"z": z, "y": y, "x": x}
    nexts = {"z": (z_next, z_last), "y": (y_next, y_last), "x": (x_next, x_last)}

    def region(o, stage, value, half=None):
        order = ORDERS[o]
        index = dict(here)
        for a in order[:stage]:
            index[a] = slice(None)
        index[order[stage]] = value
        at = (3 * core + o, index["z"], index["y"], index["x"])
        return cots.at[at if half is None else at + (half,)]

    def ring_send(o, stage, kind):
        axis = ORDERS[o][stage]
        a = here[axis]
        value = (a, a, (a + 3) % 4, (a + 1) % 4)[kind]
        ref = region(o, stage, value, None if kind < 2 else kind - 2)
        send(RING + (o * 3 + stage) * 4 + kind, ref, ref, nexts[axis][kind % 2])

    def ring_arrive(o, stage, kind):
        a = here[ORDERS[o][stage]]
        value = ((a + 3) % 4, (a + 1) % 4, (a + 2) % 4, (a + 2) % 4)[kind]
        arrive(RING + (o * 3 + stage) * 4 + kind, region(o, stage, value, None if kind < 2 else kind - 2))

    def ring_first(stage, which=(0, 1, 2)):
        for o in which:
            for kind in (0, 1):
                ring_send(o, stage, kind)

    def ring_second(stage, which=(0, 1, 2)):
        for o in which:
            for kind in (0, 1):
                ring_arrive(o, stage, kind)
                ring_send(o, stage, kind + 2)

    def ring_end(stage, which=(0, 1, 2)):
        for o in which:
            for kind in (2, 3):
                ring_arrive(o, stage, kind)

    def plane_send(o, by):
        ref = cots.at[3 * core + o, (z + by) % 4]
        send(PLANE + o * 4 + by, ref, ref, sibling)

    def plane_arrive(o, by):
        arrive(PLANE + o * 4 + by, cots.at[3 * other + o, (z + by) % 4])

    def sum_cores(base, parts, pair):
        send(base, parts.at[other], pair, sibling)

    def sum_x(base, parts, pair, held, one):
        arrive(base, pair)
        for h in range(2):
            for i in range(4):
                held[i, h] = (parts[core, h, i].astype(F32) + pair[h, i].astype(F32)).astype(BF16)
        send(base + 1, held.at[far, 0], one.at[0], x_next)
        send(base + 2, held.at[far, 1], one.at[1], x_last)

    def sum_x_more(base, held, one, two):
        for h, to, at in ((0, x_next, ahead), (1, x_last, behind)):
            arrive(base + 1 + h, one.at[h])
            held[at, h] = (held[at, h].astype(F32) + one[h].astype(F32)).astype(BF16)
            send(base + 3 + h, held.at[at], two.at[h], to)

    def sum_of(held, two, h):
        return held[x, h].astype(F32) + two[0, h].astype(F32) + two[1, h].astype(F32)

    def sum_y(base, held, two, cross):
        for h in range(2):
            arrive(base + 3 + h, two.at[h])
        cross[0] = sum_of(held, two, 1 - y_hi).astype(BF16)
        send(base + 5, cross.at[0], cross.at[1], y_peer)

    def sum_end(base, held, two, cross):
        arrive(base + 5, cross.at[1])
        return sum_of(held, two, y_hi) + cross[1].astype(F32)

    feats_copy.wait()
    group = 4
    block = group * rows

    def spread_block(i):
        plus = feats[:, pl.ds(pl.multiple_of(i * block, block), block)]
        minus = feats[:, pl.ds(pl.multiple_of(width + i * block, block), block)]
        part = dot(plus, spread_ref[0], ((0,), (0,))) + dot(minus, spread_ref[1], ((0,), (0,)))
        part = part.astype(BF16)
        for g in range(group):
            x_parts[g % 2, i // 2, i % 2 * 2 + g // 2] = part[g * rows : (g + 1) * rows]

    span(0, width // block, spread_block)
    sum_cores(X_SUM, x_parts, x_pair)
    arrive(SWAP, cots.at[pl.ds(3 * core, 3), z, y, x, other])
    ring_first(0)

    def merge(t):
        weight_copy(t).wait()
        total = jnp.zeros((double, LANES), F32)
        for k in range(experts):
            total += coefs_ref[d, k] * weights[t, k].astype(F32)
        merged[:, pl.ds(pl.multiple_of(t * LANES, LANES), LANES)] = total.astype(BF16)

    span(0, tiles // 4, merge)
    sum_x(X_SUM, x_parts, x_pair, x_held, x_one)
    ring_second(0)
    span(tiles // 4, tiles // 2, merge)
    sum_x_more(X_SUM, x_held, x_one, x_two)
    ring_end(0)
    ring_first(1)
    span(tiles // 2, 3 * tiles // 4, merge)
    sum_y(X_SUM, x_held, x_two, x_cross)
    ring_second(1)
    span(3 * tiles // 4, tiles, merge)
    ring_end(1, (2,))
    ring_first(2, (2,))
    ring_end(1, (0, 1))
    ring_first(2, (0, 1))
    for o in range(2):
        plane_send(o, 0)

    x_here = sum_end(X_SUM, x_held, x_two, x_cross).astype(BF16)
    x_all[d] = x_here
    send(X_DP, x_all.at[d], x_all.at[d], lo_peer)
    x_wide = x_here.astype(F32)
    both = interleave(wide, x_wide, -turn(x_wide))
    both_turned = both.T.astype(BF16)
    both = both.astype(BF16)

    def out_block(i):
        cols = pl.ds(pl.multiple_of(i * block, block), block)
        part = dot(both_turned, merged[:, cols], ((1,), (0,))).astype(BF16)
        for p in range(MP):
            out_parts[p % 2, p // 8, p // 2 % 4, :, cols] = part[p * 16 : (p + 1) * 16]

    span(0, width // block, out_block)
    sum_cores(OUT_SUM, out_parts, out_pair)

    pair = x_all.at[pl.ds(2 * z, 2)]
    arrive(X_DP, x_all.at[d + 1 - 2 * y_lo])
    send(X_DP + 1, pair, pair, z_next)
    send(X_DP + 2, pair, pair, z_last)

    sum_x(OUT_SUM, out_parts, out_pair, out_held, out_one)
    ring_second(2, (2,))
    sum_x_more(OUT_SUM, out_held, out_one, out_two)

    for h, to, by in ((0, z_next, 3), (1, z_last, 1)):
        arrive(X_DP + 1 + h, x_all.at[pl.ds((z + by) % 4 * 2, 2)])
        ref = x_all.at[(z + by) % 4 * 2 + h]
        send(X_DP + 3 + h, ref, ref, to)

    ring_end(2, (2,))
    for by in range(4):
        plane_send(2, by)
    sum_y(OUT_SUM, out_held, out_two, out_cross)

    for o in range(3):
        plane_arrive(o, 0)
    for s in range(SLICES):
        for h in range(2):
            crystal[h * LANES : (h + 1) * LANES, s * COLS : (s + 1) * COLS] = cots[s, z, y_lo + 2 * h].reshape(
                LANES, COLS
            )
    by_real, by_imag = separate(wide, dot(merged[...], crystal[...], ((1,), (1,))))
    back_all[y_hi, x, core] = (by_real + turn(by_imag)).astype(BF16)
    low = 1 - y_hi
    mine_back = back_all.at[y_hi, x, core]
    send(BACK, mine_back, mine_back, y_peer)
    send(BACK + 1, mine_back, mine_back, x_next)
    send(BACK + 2, mine_back, mine_back, x_last)
    ring_second(2, (0, 1))
    peer_back = back_all.at[low, x, core]
    arrive(BACK, peer_back)
    send(BACK + 3, peer_back, peer_back, x_next)
    send(BACK + 4, peer_back, peer_back, x_last)

    def coef_add(t, sums):
        cols = pl.ds(pl.multiple_of(t * LANES, LANES), LANES)
        grad = dot(both, crystal[:, cols], ((1,), (0,))) * norm
        added = []
        for k in range(experts):
            terms = weights[t, k].astype(F32) * grad
            added.append(sums[k] + jnp.sum(terms.reshape(-1, 8, LANES), 0))
        return tuple(added)

    sums = tuple(jnp.zeros((8, LANES), F32) for _ in range(experts))
    sums = lax.fori_loop(0, tiles // 2, coef_add, sums)
    arrive(BACK + 1, back_all.at[y_hi, behind, core])
    send(BACK + 5, back_all.at[y_hi, behind, core], back_all.at[y_hi, behind, core], x_next)
    arrive(BACK + 4, back_all.at[low, ahead, core])
    send(BACK + 6, back_all.at[low, ahead, core], back_all.at[low, ahead, core], x_last)
    sums = lax.fori_loop(tiles // 2, tiles, coef_add, sums)
    lanes = jnp.sum(jnp.concatenate([jnp.sum(v, 0, keepdims=True) for v in sums], 0), 1, keepdims=True)
    same = lax.broadcasted_iota(jnp.int32, (experts, LANES), 0) == lax.broadcasted_iota(
        jnp.int32, (experts, LANES), 1
    )
    coef_parts[0] = jnp.sum(jnp.where(same, lanes, 0.0), 0, keepdims=True)

    def coef_copy(j):
        sem = COEF + j - 1
        return remote(coef_parts.at[0], coef_parts.at[j], send_sem.at[sem], recv_sem.at[sem], mp_peer(j))

    span(1, MP, lambda j: coef_copy(j).start())

    out = sum_end(OUT_SUM, out_held, out_two, out_cross)
    half = out.shape[0] // 2
    atom_ref[...] = jnp.concatenate([out[:half], out[half:]], 1).astype(BF16)

    arrive(BACK + 2, back_all.at[y_hi, ahead, core])
    arrive(BACK + 3, back_all.at[low, behind, core])
    arrive(BACK + 5, back_all.at[y_hi, far, core])
    arrive(BACK + 6, back_all.at[low, far, core])
    send(BACK + 7, back_all.at[0, :, core], back_all.at[0, :, core], sibling)
    send(BACK + 8, back_all.at[1, :, core], back_all.at[1, :, core], sibling)

    ring_end(2, (0, 1))
    for by in range(1, 4):
        for o in range(2):
            plane_send(o, by)

    stores = []

    def store(src, dst):
        copy = pltpu.make_async_copy(src, dst, store_sem.at[len(stores)])
        copy.start()
        stores.append(copy)

    for o in range(3):
        store(cots.at[3 * core + o], cot_hbm.at[3 * core + o])
    for h, by in ((0, 3), (1, 1)):
        arrive(X_DP + 3 + h, x_all.at[(z + 2) % 4 * 2 + h])
    store(x_all, x_hbm)
    arrive(BACK + 7, back_all.at[0, :, other])
    arrive(BACK + 8, back_all.at[1, :, other])
    store(back_all, back_hbm)

    span(1, MP, lambda j: coef_copy(j).wait_recv())
    coef_ref[...] = jnp.sum(coef_parts[...], 0)[:, :experts] * (width**-0.5)

    for by in range(4):
        for o in range(3):
            if by > 0:
                plane_arrive(o, by)
            at = (3 * other + o, (z + by) % 4)
            store(cots.at[at], cot_hbm.at[at])

    span(1, MP, lambda j: coef_copy(j).wait_send())
    for copy in sent:
        copy.wait_send()
    for copy in stores:
        copy.wait()


def exchange(edge_feats, targets, roll_ids, counts, coefs, weights, roll_angles, atom_cot):
    slots, wide = edge_feats.shape
    width = wide // 2
    experts, rows = weights.shape[:2]
    atoms_here = atom_cot.shape[0]
    q = 2 * MP * atoms_here
    vmem = pl.BlockSpec(memory_space=pltpu.VMEM)
    smem = pl.BlockSpec(memory_space=pltpu.SMEM)
    hbm = pl.BlockSpec(memory_space=pl.ANY)
    dma = pltpu.SemaphoreType.DMA
    cots = (SLICES, 4, 4, 4, 2, 16, COLS)
    sums = [
        pltpu.VMEM(lead + block, BF16)
        for block in ((rows, q), (16, width))
        for lead in ((2, 2, 4), (2, 4), (4, 2), (2,), (2, 2), (2,))
    ]
    return pl.pallas_call(
        functools.partial(exchange_kernel, (atoms_here / slots) ** 0.5, (slots * MP) ** -0.5),
        in_specs=[hbm, vmem, vmem, smem, smem, hbm, vmem, vmem],
        out_specs=[vmem, vmem, vmem, hbm, hbm, hbm],
        out_shape=[
            jax.ShapeDtypeStruct(atom_cot.shape, BF16),
            jax.ShapeDtypeStruct((1, experts), F32),
            jax.ShapeDtypeStruct((2, slots, q), BF16),
            jax.ShapeDtypeStruct((DP, rows, q), BF16),
            jax.ShapeDtypeStruct((2, 4, 2, rows, q), BF16),
            jax.ShapeDtypeStruct(cots, BF16),
        ],
        scratch_shapes=[
            pltpu.VMEM(edge_feats.shape, BF16),
            pltpu.VMEM((width // LANES, experts, 2 * rows, LANES), BF16),
            pltpu.VMEM((2 * rows, width), BF16),
            pltpu.VMEM((SLICES, 16, COLS), BF16),
            pltpu.VMEM((q, width), BF16),
            pltpu.VMEM(cots, BF16),
            pltpu.VMEM((DP, rows, q), BF16),
            pltpu.VMEM((2, 4, 2, rows, q), BF16),
            pltpu.VMEM((MP, 1, LANES), F32),
            pltpu.VMEM((2, 2 * rows, LANES), F32),
            *sums,
            dma(()), dma((width // LANES,)), dma((17,)), dma((COPIES,)), dma((COPIES,)),
        ],
        compiler_params=pltpu.CompilerParams(
            collective_id=0, has_side_effects=True, vmem_limit_bytes=56 * 2**20
        ),
        cost_estimate=pl.CostEstimate(flops=4 * 10**9, bytes_accessed=2 * 10**7, transcendentals=0),
    )(
        edge_feats, targets[None], roll_ids[None], counts, coefs, weights, roll_angles[None], atom_cot
    )


def mix_kernel(norm, coefs_ref, x_ref, cot_ref, back_ref, spread_ref, wg_hbm, eg_ref, both_ref, wide, gm_ref, left_ref,
               out_ref, sem):
    step, steps = pl.program_id(0), pl.num_programs(0)
    crystals, rows, _ = x_ref.shape
    experts, _, _, width = wg_hbm.shape
    wg_rows = wg_hbm.reshape(experts, 2 * rows, width)

    @pl.when(step == 0)
    def _():
        r = lax.broadcasted_iota(jnp.int32, (16 * experts, 16 * crystals), 0)
        c = lax.broadcasted_iota(jnp.int32, (16 * experts, 16 * crystals), 1)
        pieces = []
        for k in range(experts):
            row = jnp.zeros((16, 16 * crystals), F32)
            for i in range(crystals):
                row = jnp.where(c[:16] // 16 == i, coefs_ref[i, k], row)
            pieces.append(row)
        mixed = jnp.where(r % 16 == c % 16, jnp.concatenate(pieces, 0), 0.0)
        high = mixed.astype(BF16)
        left_ref[:, : 16 * crystals] = high
        left_ref[:, 16 * crystals :] = (mixed - high.astype(F32)).astype(BF16)
        for i in range(crystals):
            x = x_ref[i].astype(F32)
            both_ref[i] = interleave(wide, x, -turn(x)).astype(BF16)

    for i in range(crystals):
        cot = jnp.concatenate(
            [cot_ref[0, i // 2, i % 2 + 2 * h].reshape(LANES, COLS) for h in range(2)], 0
        )
        gm_ref[i] = (dot(both_ref[i], cot, ((1,), (0,))) * norm).astype(BF16)

    slot = lax.rem(step, 2)

    def copies(step):
        slot = lax.rem(step, 2)
        return [
            pltpu.make_async_copy(
                out_ref.at[slot, t],
                wg_rows.at[:, :, pl.ds(pl.multiple_of(step * COLS + t * LANES, LANES), LANES)],
                sem.at[slot, t],
            )
            for t in range(2)
        ]

    @pl.when(step >= 2)
    def _():
        for copy in copies(step - 2):
            copy.wait()

    for g in range(2 * rows // 16):
        right = jnp.concatenate([gm_ref[i, g * 16 : (g + 1) * 16, :] for i in range(crystals)] * 2, 0)
        out = dot(left_ref[...], right, ((1,), (0,))).astype(BF16)
        for t in range(2):
            for k in range(experts):
                piece = out[k * 16 : (k + 1) * 16, t * LANES : (t + 1) * LANES]
                out_ref[slot, t, k, g * 16 : (g + 1) * 16] = piece

    for copy in copies(step):
        copy.start()

    part = step // (steps // 2)
    cols = eg_ref.shape[1]
    at = pl.multiple_of(step % (steps // 2) * cols, cols)
    eg_ref[...] = dot(spread_ref[part], back_ref[pl.ds(at, cols), :], ((1,), (1,))).astype(BF16)

    @pl.when(step == steps - 1)
    def _():
        for copy in copies(step - 1) + copies(step):
            copy.wait()


def mix(coefs, x_all, cot_all, back_all, spread, norm):
    crystals, experts = coefs.shape
    _, rows, q = x_all.shape
    width = back_all.shape[0]
    slots = spread.shape[1]
    whole = lambda shape: pl.BlockSpec(shape, lambda i: (0,) * len(shape))
    return pl.pallas_call(
        functools.partial(mix_kernel, norm),
        grid=(SLICES,),
        in_specs=[
            pl.BlockSpec(memory_space=pltpu.SMEM),
            whole(x_all.shape),
            pl.BlockSpec((1,) + cot_all.shape[1:], lambda i: (i,) + (0,) * 6),
            whole(back_all.shape),
            whole(spread.shape),
        ],
        out_specs=[
            pl.BlockSpec(memory_space=pl.ANY),
            pl.BlockSpec((slots, 2 * width // SLICES), lambda i: (0, i)),
        ],
        out_shape=[
            jax.ShapeDtypeStruct((experts, rows, 2, width), BF16),
            jax.ShapeDtypeStruct((slots, 2 * width), BF16),
        ],
        scratch_shapes=[
            pltpu.VMEM((crystals, 2 * rows, q), BF16),
            pltpu.VMEM((2, 2 * rows, LANES), F32),
            pltpu.VMEM((crystals, 2 * rows, COLS), BF16),
            pltpu.VMEM((16 * experts, 32 * crystals), BF16),
            pltpu.VMEM((2, 2, experts, 2 * rows, LANES), BF16),
            pltpu.SemaphoreType.DMA((2, 2)),
        ],
        compiler_params=pltpu.CompilerParams(vmem_limit_bytes=60 * 2**20),
        cost_estimate=pl.CostEstimate(flops=10**10, bytes_accessed=2 * 10**7, transcendentals=0),
    )(coefs, x_all, cot_all, back_all, spread)


def on_device(edge_feats, targets, roll_ids, counts, coefs, weights, roll_angles, atom_cot):
    slots = edge_feats.shape[0]
    atom_out, coef_grad, spread, x_all, back_all, cot_all = exchange(
        edge_feats, targets, roll_ids, counts, coefs, weights, roll_angles, atom_cot
    )
    back_all = back_all.reshape(-1, back_all.shape[-1])
    weight_grad, edge_grad = mix(coefs, x_all, cot_all, back_all, spread, (slots * MP) ** -0.5)
    return (atom_out, edge_grad, weight_grad, coef_grad)


def solution(mesh):
    placed = (
        P(("dp", "mp"), None),
        P(("dp", "mp")),
        P(("dp", "mp")),
        P(("dp", "mp")),
        P(),
        P(None, "mp", None, None),
        P(),
        P(("dp", "mp"), None),
    )
    return jax.shard_map(
        on_device,
        mesh=mesh,
        in_specs=placed,
        out_specs=(
            P(("dp", "mp"), None),
            P(("dp", "mp"), None),
            P(None, "mp", None, None),
            P("dp", None),
        ),
        check_vma=False,
    )
```

time: 101 us -> 74.5 us (0.74)
  Pallas kernels: 92.4 us -> 71.7 us
  local copies, waits for them, and re-layouts: 7 us -> 1.14 us
    pallas_call x1, Pallas kernels: 79.3 us -> 59.8 us  [exchange(): pl.pallas_call(functools.partial(exchange_kernel, (atoms_here / slots) **...]
    unnamed x16 -> x6, local copies, waits for them, and re-layouts: 7 us -> 1.14 us
    pallas_call x1, Pallas kernels: 13 us -> 11.9 us  [mix(): pl.pallas_call(functools.partial(mix_kernel, norm), grid=(SLICES,), in_sp...]
where the time goes in v3:
time: 74.5 us; the launch traced here: 74.2 us
  Pallas kernels  71.7 us (96%)
  between operations  1.32 us (2%)
  local copies, waits for them, and re-layouts  1.14 us (2%)
    pallas_call x1, Pallas kernels, exchange(): pl.pallas_call(functools.partial(exchange_kernel, (atoms_here / slots) **...  59.8 us
    pallas_call x1, Pallas kernels, mix(): pl.pallas_call(functools.partial(mix_kernel, norm), grid=(SLICES,), in_sp...  11.9 us

profile of v3, /device:TPU:1, one launch (start us, length us, event | category | flops | bytes accessed | tf_op | source)
XLA Modules:
  0.0 74.2 jit_solution(18099660584493267967)
XLA Ops:
  1.3 59.8 %shard_map.111 = (bf16[8,3072]{1,0:T(8,128)(2,1)}, f32[1,16]{1,0:T(1,128)}, bf16[2,256,256]{2,1,0:T(8,128)(2,1)}, bf16[8,96,256]{2,1,0:T(8,128)(2,1)}, bf16[2,4,...) custom-call(bf16[256,3072]{1,0:T(8,128)(2,1)} %feats_hbm.1, s32[1,256]{1,0:T(1,128)} %bitcast.4, ...), custom_call_target="tpu_custom_call" | custom-call | flops 4000000000 | bytes 20000000 | tf_op jit(solution)/shard_map/pallas_call | solution.py:410
  61.0 0.0 copy-start
  61.1 0.0 copy-start.1
  61.1 11.9 %shard_map.112 = (bf16[16,96,2,1536]{3,2,1,0:T(2,128)(2,1)}, bf16[256,3072]{1,0:T(8,128)(2,1)}) custom-call(f32[8,16]{1,0:T(8,128)} %coefs_ref.3, bf16[8,96,256]{2,1,0:T(8,128)(2,1)} %get-tuple-element.13.x_ref, bf16[6,4,4,4,2,16,256]{6,5,4,3,2,1,0:T(8,128)(2,1)} %get-tuple-element.14.cot_ref, bf16[1536,256]{1,0:T(8,128)(2,1)} %bitcast.7, ...), custom_call_target="tpu_custom_call" | custom-call | flops 10000000000 | bytes 20000000 | tf_op jit(solution)/shard_map/pallas_call | solution.py:522
  73.0 0.0 copy-done
  73.0 0.6 copy.15
  73.6 0.0 copy-done.1
  73.6 0.5 copy.16
Async XLA Ops:
  61.0 12.0 %copy-start = (bf16[8,3072]{1,0:T(8,128)(2,1)S(1)}, bf16[8,3072]{1,0:T(8,128)(2,1)}, u32[]{:S(2)}) copy-start(bf16[8,3072]{1,0:T(8,128)(2,1)} %get-tuple-element.24) | copy-start | bytes 147460
  61.1 12.6 %copy-start.1 = (f32[1,16]{1,0:T(1,128)S(1)}, f32[1,16]{1,0:T(1,128)}, u32[]{:S(2)}) copy-start(f32[1,16]{1,0:T(1,128)} %get-tuple-element.27) | copy-start | bytes 196

commit v4 on v3

v4 whole, which is shorter than its diff:
```python
import functools

import jax
import jax.numpy as jnp
from jax import lax
from jax.experimental import pallas as pl
from jax.experimental.pallas import tpu as pltpu
from jax.sharding import PartitionSpec as P

BF16, F32 = jnp.bfloat16, jnp.float32
LANES = 128
MESH = pl.DeviceIdType.MESH
DP, MP = 8, 16
SLICES, COLS = 6, 256
ORDERS = (("x", "y", "z"), ("z", "x", "y"), ("y", "z", "x"))
SWAP, RING, PLANE, X_SUM, OUT_SUM, COT, BACK, X_DP, COEF = 0, 1, 28, 40, 48, 56, 64, 72, 76
COPIES = COEF + MP - 1


def dot(a, b, contract):
    return lax.dot_general(a, b, (contract, ((), ())), preferred_element_type=F32)


def turn(rows):
    n = rows.shape[1]
    col = lax.broadcasted_iota(jnp.int32, rows.shape, 1)
    return jnp.where(col // 8 % 2 == 0, pltpu.roll(rows, n - 8, 1), -pltpu.roll(rows, 8, 1))


def interleave(wide, even, odd):
    n = even.shape[0]
    for h in range(2):
        wide[h, pl.ds(0, n, stride=2), :] = even[:, h * LANES : (h + 1) * LANES]
        wide[h, pl.ds(1, n, stride=2), :] = odd[:, h * LANES : (h + 1) * LANES]
    return jnp.concatenate([wide[0], wide[1]], 1)


def separate(wide, both):
    n = both.shape[0] // 2
    for h in range(2):
        wide[h] = both[:, h * LANES : (h + 1) * LANES]
    return [
        jnp.concatenate([wide[h, pl.ds(part, n, stride=2), :] for h in range(2)], 1) for part in range(2)
    ]


def remote(src, dst, send, recv, target):
    return pltpu.make_async_remote_copy(
        src_ref=src, dst_ref=dst, send_sem=send, recv_sem=recv, device_id=target, device_id_type=MESH
    )


def column_of(row):
    n = row.shape[1]
    same = lax.broadcasted_iota(jnp.int32, (n, n), 0) == lax.broadcasted_iota(jnp.int32, (n, n), 1)
    return jnp.sum(jnp.where(same, row, 0.0), 1, keepdims=True)


def exchange_kernel(
    scale, norm,
    feats_hbm, targets_ref, rolls_ref, counts_ref, coefs_ref, weights_hbm, angles_ref, cot_ref,
    atom_ref, coef_ref, spread_ref, left_ref, both_hbm, back_hbm, cot_hbm,
    feats, weights, merged, mine, crystal, cots, x_all, both_all, back_all, coef_parts, wide,
    x_parts, x_pair, x_held, x_slots, x_cross, out_parts, out_pair, out_held, out_slots, out_cross,
    load_sem, weight_sem, store_sem, send_sem, recv_sem,
):
    d, m = lax.axis_index("dp"), lax.axis_index("mp")
    z, y, x, core = d // 2, m // 8 * 2 + d % 2, m // 2 % 4, m % 2
    y_hi, y_lo = m // 8, d % 2
    tiles, experts, double, _ = weights.shape
    rows, width = double // 2, tiles * LANES
    other = 1 - core
    ahead, behind, far = (x + 1) % 4, (x + 3) % 4, (x + 2) % 4

    def device(z, y, x, core):
        return (z * 2 + y % 2, y // 2 * 8 + x * 2 + core)

    sibling = device(z, y, x, other)
    x_next, x_last = device(z, y, ahead, core), device(z, y, behind, core)
    y_peer = device(z, (y + 2) % 4, x, core)
    x_far, z_far = device(z, y, far, core), device((z + 2) % 4, y, x, core)
    z_next, z_last = device((z + 1) % 4, y, x, core), device((z + 3) % 4, y, x, core)
    y_next, y_last = device(z, (y + 1) % 4, x, core), device(z, (y + 3) % 4, x, core)
    lo_peer = (d + 1 - 2 * y_lo, m)

    def mp_peer(j):
        return (d, lax.rem(m + j, MP))

    def span(start, stop, body):
        lax.fori_loop(start, stop, lambda j, c: (body(j), c)[1], 0)

    barrier = pltpu.get_barrier_semaphore()
    span(1, MP, lambda j: pl.semaphore_signal(barrier, inc=1, device_id=mp_peer(j), device_id_type=MESH))
    for to in (z_next, z_last, z_far, y_next, y_last):
        pl.semaphore_signal(barrier, inc=1, device_id=to, device_id_type=MESH)

    feats_copy = pltpu.make_async_copy(feats_hbm, feats, load_sem)
    feats_copy.start()
    weight_rows = weights_hbm.reshape(experts, double, width)

    def weight_copy(t):
        cols = pl.ds(pl.multiple_of(t * LANES, LANES), LANES)
        return pltpu.make_async_copy(weight_rows.at[:, :, cols], weights.at[t], weight_sem.at[t])

    span(0, tiles, lambda t: weight_copy(t).start())

    sent = []

    def send(sem, src, dst, to):
        copy = remote(src, dst, send_sem.at[sem], recv_sem.at[sem], to)
        copy.start()
        sent.append(copy)

    def arrive(sem, ref):
        remote(ref, ref, send_sem.at[sem], recv_sem.at[sem], sibling).wait_recv()

    c = cot_ref[...].astype(F32)
    own = jnp.concatenate([c[:, :width], c[:, width:]], 0).astype(BF16)
    crystal[y_hi, x, core] = own
    for s in range(SLICES):
        mine[s] = own[:, s * COLS : (s + 1) * COLS]
    for o in range(3):
        cots[3 * core + o, z, y, x, core] = mine[3 * core + o]

    slots = targets_ref.shape[1]
    table = rolls_ref[...] == lax.broadcasted_iota(jnp.int32, (angles_ref.shape[1], slots), 0)
    angle = column_of(angles_ref[...])
    valid = lax.broadcasted_iota(jnp.int32, (1, slots), 1) < counts_ref[0]
    factor = jnp.where(valid, scale, 0.0)
    cosine = column_of(jnp.sum(jnp.where(table, jnp.cos(angle), 0.0), 0, keepdims=True) * factor)
    sine = column_of(jnp.sum(jnp.where(table, jnp.sin(angle), 0.0), 0, keepdims=True) * factor)
    target = column_of(targets_ref[...].astype(F32)).astype(jnp.int32)
    q = lax.broadcasted_iota(jnp.int32, (slots, spread_ref.shape[2]), 1)
    hit = target == q // 16 * 8 + q % 8
    real = q // 8 % 2 == 0
    spread_ref[0] = jnp.where(hit, jnp.where(real, cosine, sine), 0.0).astype(BF16)
    spread_ref[1] = jnp.where(hit, jnp.where(real, -sine, cosine), 0.0).astype(BF16)

    pl.semaphore_wait(barrier, MP - 1 + 5)

    theirs = pl.ds(3 * other, 3)
    send(SWAP, mine.at[theirs], cots.at[theirs, z, y, x, core], sibling)

    here = {"z": z, "y": y, "x": x}
    nexts = {"z": (z_next, z_last, z_far), "y": (y_next, y_last, y_peer), "x": (x_next, x_last, x_far)}

    def region(o, stage, by, whose):
        order = ORDERS[o]
        index = dict(here)
        for a in order[:stage]:
            index[a] = slice(None)
        index[order[stage]] = (here[order[stage]] + by) % 4
        return cots.at[3 * whose + o, index["z"], index["y"], index["x"]]

    def ring_send(stage):
        for o in range(3):
            ref = region(o, stage, 0, core)
            for i, to in enumerate(nexts[ORDERS[o][stage]]):
                send(RING + (o * 3 + stage) * 3 + i, ref, ref, to)

    def ring_arrive(o, stage, i):
        arrive(RING + (o * 3 + stage) * 3 + i, region(o, stage, (3, 1, 2)[i], core))

    def ring_all(stage):
        for o in range(3):
            for i in range(3):
                ring_arrive(o, stage, i)

    def plane_send(o, by):
        ref = region(o, 2, by, core)
        send(PLANE + o * 4 + by, ref, ref, sibling)

    def plane_arrive(o, by):
        arrive(PLANE + o * 4 + by, region(o, 2, by, other))

    low = 1 - y_hi
    along = ((x_next, ahead), (x_last, behind), (x_far, far))

    def sum_cores(base, parts, pair):
        send(base, parts.at[other], pair, sibling)

    def sum_x(base, parts, pair, held, slots):
        arrive(base, pair)
        for n, h in enumerate((low, y_hi)):
            for i in range(4):
                held[i, h] = (parts[core, h, i].astype(F32) + pair[h, i].astype(F32)).astype(BF16)
            for i, (to, at) in enumerate(along):
                send(base + 1 + 3 * n + i, held.at[at, h], slots.at[n, i], to)

    def sum_of(base, held, slots, n, h):
        total = held[x, h].astype(F32)
        for i in range(3):
            arrive(base + 1 + 3 * n + i, slots.at[n, i])
            total += slots[n, i].astype(F32)
        return total

    def sum_y(base, held, slots, cross):
        cross[0] = sum_of(base, held, slots, 0, low).astype(BF16)
        send(base + 7, cross.at[0], cross.at[1], y_peer)

    def sum_end(base, held, slots, cross):
        total = sum_of(base, held, slots, 1, y_hi)
        arrive(base + 7, cross.at[1])
        return total + cross[1].astype(F32)

    def gather_first(base, ref):
        own = ref.at[y_hi, x, core]
        for i, to in enumerate((y_peer, x_next, x_last, x_far)):
            send(base + i, own, own, to)

    def gather_second(base, ref):
        got = ref.at[low, x, core]
        arrive(base, got)
        for i, (to, _) in enumerate(along):
            send(base + 4 + i, got, got, to)

    def gather_cores(base, ref):
        for n, h in enumerate((y_hi, low)):
            for i, at in enumerate((behind, ahead, far)):
                arrive(base + 1 + 3 * n + i, ref.at[h, at, core])
        ours = ref.at[:, :, core]
        send(base + 7, ours, ours, sibling)

    def gather_end(base, ref):
        arrive(base + 7, ref.at[:, :, other])

    gather_first(COT, crystal)

    feats_copy.wait()
    group = 4
    block = group * rows

    def spread_block(i):
        plus = feats[:, pl.ds(pl.multiple_of(i * block, block), block)]
        minus = feats[:, pl.ds(pl.multiple_of(width + i * block, block), block)]
        part = dot(plus, spread_ref[0], ((0,), (0,))) + dot(minus, spread_ref[1], ((0,), (0,)))
        part = part.astype(BF16)
        for g in range(group):
            x_parts[g % 2, i // 2, i % 2 * 2 + g // 2] = part[g * rows : (g + 1) * rows]

    span(0, width // block, spread_block)
    sum_cores(X_SUM, x_parts, x_pair)
    arrive(SWAP, cots.at[pl.ds(3 * core, 3), z, y, x, other])
    ring_send(0)
    sum_x(X_SUM, x_parts, x_pair, x_held, x_slots)
    gather_second(COT, crystal)

    def merge(t):
        weight_copy(t).wait()
        total = jnp.zeros((double, LANES), F32)
        for k in range(experts):
            total += coefs_ref[d, k] * weights[t, k].astype(F32)
        merged[:, pl.ds(pl.multiple_of(t * LANES, LANES), LANES)] = total.astype(BF16)

    span(0, tiles // 3, merge)
    ring_all(0)
    ring_send(1)
    sum_y(X_SUM, x_held, x_slots, x_cross)
    span(tiles // 3, 2 * tiles // 3, merge)
    gather_cores(COT, crystal)
    span(2 * tiles // 3, tiles, merge)

    gather_end(COT, crystal)
    by_real, by_imag = separate(wide, dot(merged[...], crystal[...].reshape(-1, width), ((1,), (1,))))
    back_all[y_hi, x, core] = (by_real + turn(by_imag)).astype(BF16)
    gather_first(BACK, back_all)

    x_here = sum_end(X_SUM, x_held, x_slots, x_cross).astype(BF16)
    x_all[d] = x_here
    send(X_DP, x_all.at[d], x_all.at[d], lo_peer)
    x_wide = x_here.astype(F32)
    both = interleave(wide, x_wide, -turn(x_wide))
    both_turned = both.T.astype(BF16)
    both = both.astype(BF16)

    def out_block(i):
        cols = pl.ds(pl.multiple_of(i * block, block), block)
        part = dot(both_turned, merged[:, cols], ((1,), (0,))).astype(BF16)
        for p in range(MP):
            out_parts[p % 2, p // 8, p // 2 % 4, :, cols] = part[p * 16 : (p + 1) * 16]

    span(0, width // block, out_block)
    sum_cores(OUT_SUM, out_parts, out_pair)

    ring_all(1)
    ring_send(2)
    for o in range(3):
        plane_send(o, 0)
    gather_second(BACK, back_all)
    sum_x(OUT_SUM, out_parts, out_pair, out_held, out_slots)
    pair = x_all.at[pl.ds(2 * z, 2)]
    arrive(X_DP, x_all.at[d + 1 - 2 * y_lo])
    for i, to in enumerate((z_next, z_last, z_far)):
        send(X_DP + 1 + i, pair, pair, to)

    def coef_add(t, sums):
        cols = pl.ds(pl.multiple_of(t * LANES, LANES), LANES)
        grad = dot(both, crystal[:, :, :, :, cols].reshape(-1, LANES), ((1,), (0,))) * norm
        added = []
        for k in range(experts):
            terms = weights[t, k].astype(F32) * grad
            added.append(sums[k] + jnp.sum(terms.reshape(-1, 8, LANES), 0))
        return tuple(added)

    sums = tuple(jnp.zeros((8, LANES), F32) for _ in range(experts))
    sums = lax.fori_loop(0, tiles // 2, coef_add, sums)
    sum_y(OUT_SUM, out_held, out_slots, out_cross)
    sums = lax.fori_loop(tiles // 2, tiles, coef_add, sums)
    lanes = jnp.sum(jnp.concatenate([jnp.sum(v, 0, keepdims=True) for v in sums], 0), 1, keepdims=True)
    same = lax.broadcasted_iota(jnp.int32, (experts, LANES), 0) == lax.broadcasted_iota(
        jnp.int32, (experts, LANES), 1
    )
    coef_parts[0] = jnp.sum(jnp.where(same, lanes, 0.0), 0, keepdims=True)

    def coef_copy(j):
        sem = COEF + j - 1
        return remote(coef_parts.at[0], coef_parts.at[j], send_sem.at[sem], recv_sem.at[sem], mp_peer(j))

    span(1, MP, lambda j: coef_copy(j).start())

    gather_cores(BACK, back_all)

    r = lax.broadcasted_iota(jnp.int32, (32, 32 * DP), 0)
    c = lax.broadcasted_iota(jnp.int32, (32, 32 * DP), 1)
    for k in range(experts):
        row = jnp.zeros((32, 32 * DP), F32)
        for i in range(DP):
            row = jnp.where(c == r + 32 * i, coefs_ref[i, k], row)
        left_ref[k * 32 : (k + 1) * 32] = row.astype(BF16)

    out = sum_end(OUT_SUM, out_held, out_slots, out_cross)
    half = out.shape[0] // 2
    atom_ref[...] = jnp.concatenate([out[:half], out[half:]], 1).astype(BF16)

    for by, i in ((3, 0), (1, 1), (2, 2)):
        arrive(X_DP + 1 + i, x_all.at[pl.ds((z + by) % 4 * 2, 2)])
    for i in range(DP):
        rows_of = x_all[i].astype(F32)
        both_all[i] = interleave(wide, rows_of, -turn(rows_of)).astype(BF16)

    stores = []

    def store(src, dst):
        copy = pltpu.make_async_copy(src, dst, store_sem.at[len(stores)])
        copy.start()
        stores.append(copy)

    store(both_all, both_hbm)
    gather_end(BACK, back_all)
    store(back_all, back_hbm)
    for i, by in enumerate((3, 1, 2)):
        for o in range(3):
            ring_arrive(o, 2, i)
            plane_send(o, by)
    for o in range(3):
        store(cots.at[3 * core + o], cot_hbm.at[3 * core + o])

    span(1, MP, lambda j: coef_copy(j).wait_recv())
    coef_ref[...] = jnp.sum(coef_parts[...], 0)[:, :experts] * (width**-0.5)

    for by in (0, 3, 1, 2):
        for o in range(3):
            plane_arrive(o, by)
            index = [slice(None)] * 3
            axis = "zyx".index(ORDERS[o][2])
            index[axis] = (here["zyx"[axis]] + by) % 4
            at = (3 * other + o, *index)
            store(cots.at[at], cot_hbm.at[at])

    span(1, MP, lambda j: coef_copy(j).wait_send())
    for copy in sent:
        copy.wait_send()
    for copy in stores:
        copy.wait()


def exchange(edge_feats, targets, roll_ids, counts, coefs, weights, roll_angles, atom_cot):
    slots, wide = edge_feats.shape
    width = wide // 2
    experts, rows = weights.shape[:2]
    atoms_here = atom_cot.shape[0]
    q = 2 * MP * atoms_here
    vmem = pl.BlockSpec(memory_space=pltpu.VMEM)
    smem = pl.BlockSpec(memory_space=pltpu.SMEM)
    hbm = pl.BlockSpec(memory_space=pl.ANY)
    dma = pltpu.SemaphoreType.DMA
    cots = (SLICES, 4, 4, 4, 2, 16, COLS)
    sums = [
        pltpu.VMEM(lead + block, BF16)
        for block in ((rows, q), (16, width))
        for lead in ((2, 2, 4), (2, 4), (4, 2), (2, 3), (2,))
    ]
    return pl.pallas_call(
        functools.partial(exchange_kernel, (atoms_here / slots) ** 0.5, (slots * MP) ** -0.5),
        in_specs=[hbm, vmem, vmem, smem, smem, hbm, vmem, vmem],
        out_specs=[vmem, vmem, vmem, vmem, hbm, hbm, hbm],
        out_shape=[
            jax.ShapeDtypeStruct(atom_cot.shape, BF16),
            jax.ShapeDtypeStruct((1, experts), F32),
            jax.ShapeDtypeStruct((2, slots, q), BF16),
            jax.ShapeDtypeStruct((32 * experts, 32 * DP), BF16),
            jax.ShapeDtypeStruct((DP, 2 * rows, q), BF16),
            jax.ShapeDtypeStruct((2, 4, 2, rows, q), BF16),
            jax.ShapeDtypeStruct(cots, BF16),
        ],
        scratch_shapes=[
            pltpu.VMEM(edge_feats.shape, BF16),
            pltpu.VMEM((width // LANES, experts, 2 * rows, LANES), BF16),
            pltpu.VMEM((2 * rows, width), BF16),
            pltpu.VMEM((SLICES, 16, COLS), BF16),
            pltpu.VMEM((2, 4, 2, 16, width), BF16),
            pltpu.VMEM(cots, BF16),
            pltpu.VMEM((DP, rows, q), BF16),
            pltpu.VMEM((DP, 2 * rows, q), BF16),
            pltpu.VMEM((2, 4, 2, rows, q), BF16),
            pltpu.VMEM((MP, 1, LANES), F32),
            pltpu.VMEM((2, 2 * rows, LANES), F32),
            *sums,
            dma(()), dma((width // LANES,)), dma((17,)), dma((COPIES,)), dma((COPIES,)),
        ],
        compiler_params=pltpu.CompilerParams(
            collective_id=0, has_side_effects=True, vmem_limit_bytes=56 * 2**20
        ),
        cost_estimate=pl.CostEstimate(flops=4 * 10**9, bytes_accessed=2 * 10**7, transcendentals=0),
    )(
        edge_feats, targets[None], roll_ids[None], counts, coefs, weights, roll_angles[None], atom_cot
    )


def mix_kernel(norm, left_ref, both_ref, cot_ref, back_ref, spread_ref, wg_hbm, eg_ref, gm_ref, out_ref, sem):
    step, steps = pl.program_id(0), pl.num_programs(0)
    crystals, double, _ = both_ref.shape
    experts, _, _, width = wg_hbm.shape
    wg_rows = wg_hbm.reshape(experts, double, width)

    for i in range(crystals):
        cot = jnp.concatenate(
            [cot_ref[0, i // 2, i % 2 + 2 * h].reshape(LANES, COLS) for h in range(2)], 0
        )
        gm_ref[i] = (dot(both_ref[i], cot, ((1,), (0,))) * norm).astype(BF16)

    slot = lax.rem(step, 2)

    def copies(step):
        slot = lax.rem(step, 2)
        return [
            pltpu.make_async_copy(
                out_ref.at[slot, t],
                wg_rows.at[:, :, pl.ds(pl.multiple_of(step * COLS + t * LANES, LANES), LANES)],
                sem.at[slot, t],
            )
            for t in range(2)
        ]

    @pl.when(step >= 2)
    def _():
        for copy in copies(step - 2):
            copy.wait()

    for g in range(double // 32):
        right = jnp.concatenate([gm_ref[i, g * 32 : (g + 1) * 32, :] for i in range(crystals)], 0)
        out = dot(left_ref[...], right, ((1,), (0,))).astype(BF16)
        for t in range(2):
            for k in range(experts):
                piece = out[k * 32 : (k + 1) * 32, t * LANES : (t + 1) * LANES]
                out_ref[slot, t, k, g * 32 : (g + 1) * 32] = piece

    for copy in copies(step):
        copy.start()

    part = step // (steps // 2)
    cols = eg_ref.shape[1]
    at = pl.multiple_of(step % (steps // 2) * cols, cols)
    eg_ref[...] = dot(spread_ref[part], back_ref[pl.ds(at, cols), :], ((1,), (1,))).astype(BF16)

    @pl.when(step == steps - 1)
    def _():
        for copy in copies(step - 1) + copies(step):
            copy.wait()


def mix(experts, left, both_all, cot_all, back_all, spread, norm):
    crystals, double, _ = both_all.shape
    width = back_all.shape[0]
    slots = spread.shape[1]
    whole = lambda shape: pl.BlockSpec(shape, lambda i: (0,) * len(shape))
    return pl.pallas_call(
        functools.partial(mix_kernel, norm),
        grid=(SLICES,),
        in_specs=[
            whole(left.shape),
            whole(both_all.shape),
            pl.BlockSpec((1,) + cot_all.shape[1:], lambda i: (i,) + (0,) * 6),
            whole(back_all.shape),
            whole(spread.shape),
        ],
        out_specs=[
            pl.BlockSpec(memory_space=pl.ANY),
            pl.BlockSpec((slots, 2 * width // SLICES), lambda i: (0, i)),
        ],
        out_shape=[
            jax.ShapeDtypeStruct((experts, double // 2, 2, width), BF16),
            jax.ShapeDtypeStruct((slots, 2 * width), BF16),
        ],
        scratch_shapes=[
            pltpu.VMEM((crystals, double, COLS), BF16),
            pltpu.VMEM((2, 2, experts, double, LANES), BF16),
            pltpu.SemaphoreType.DMA((2, 2)),
        ],
        compiler_params=pltpu.CompilerParams(vmem_limit_bytes=60 * 2**20),
        cost_estimate=pl.CostEstimate(flops=10**10, bytes_accessed=2 * 10**7, transcendentals=0),
    )(left, both_all, cot_all, back_all, spread)


def on_device(edge_feats, targets, roll_ids, counts, coefs, weights, roll_angles, atom_cot):
    slots = edge_feats.shape[0]
    atom_out, coef_grad, spread, left, both_all, back_all, cot_all = exchange(
        edge_feats, targets, roll_ids, counts, coefs, weights, roll_angles, atom_cot
    )
    back_all = back_all.reshape(-1, back_all.shape[-1])
    weight_grad, edge_grad = mix(
        weights.shape[0], left, both_all, cot_all, back_all, spread, (slots * MP) ** -0.5
    )
    return (atom_out, edge_grad, weight_grad, coef_grad)


def solution(mesh):
    placed = (
        P(("dp", "mp"), None),
        P(("dp", "mp")),
        P(("dp", "mp")),
        P(("dp", "mp")),
        P(),
        P(None, "mp", None, None),
        P(),
        P(("dp", "mp"), None),
    )
    return jax.shard_map(
        on_device,
        mesh=mesh,
        in_specs=placed,
        out_specs=(
            P(("dp", "mp"), None),
            P(("dp", "mp"), None),
            P(None, "mp", None, None),
            P("dp", None),
        ),
        check_vma=False,
    )
```

time: 74.5 us -> 69.5 us (0.933)
  Pallas kernels: 71.7 us -> 66.7 us
    pallas_call x1, Pallas kernels: 59.8 us -> 55.1 us  [exchange(): pl.pallas_call(functools.partial(exchange_kernel, (atoms_here / slots) **...]
where the time goes in v4:
time: 69.5 us; the launch traced here: 69.2 us
  Pallas kernels  66.7 us (96%)
  between operations  1.32 us (2%)
  local copies, waits for them, and re-layouts  1.14 us (2%)
    pallas_call x1, Pallas kernels, exchange(): pl.pallas_call(functools.partial(exchange_kernel, (atoms_here / slots) **...  55.1 us
    pallas_call x1, Pallas kernels, mix(): pl.pallas_call(functools.partial(mix_kernel, norm), grid=(SLICES,), in_sp...  11.6 us

profile of v4, /device:TPU:1, one launch (start us, length us, event | category | flops | bytes accessed | tf_op | source)
XLA Modules:
  0.0 69.2 jit_solution(17806284861847357633)
XLA Ops:
  1.3 55.1 %shard_map.111 = (bf16[8,3072]{1,0:T(8,128)(2,1)}, f32[1,16]{1,0:T(1,128)}, bf16[2,256,256]{2,1,0:T(8,128)(2,1)}, bf16[512,256]{1,0:T(8,128)(2,1)}, bf16[8,192,2...) custom-call(bf16[256,3072]{1,0:T(8,128)(2,1)} %feats_hbm.1, ...), custom_call_target="tpu_custom_call" | custom-call | flops 4000000000 | bytes 20000000 | tf_op jit(solution)/shard_map/pallas_call | solution.py:393
  56.4 0.0 copy-start
  56.4 0.0 copy-start.1
  56.4 11.6 %shard_map.112 = (bf16[16,96,2,1536]{3,2,1,0:T(2,128)(2,1)}, bf16[256,3072]{1,0:T(8,128)(2,1)}) custom-call(bf16[512,256]{1,0:T(8,128)(2,1)} %get-tuple-element.14.left_ref, bf16[8,192,256]{2,1,0:T(8,128)(2,1)} %get-tuple-element.15.both_ref, bf16[6,4,4,4,2,16,256]{6,5,4,3,2,1,0:T(8,128)(2,1)} %get-tuple-element.16.cot_ref, bf16[1536,256]{1,0:T(8,128)(2,1)} %bitcast.7, ...), custom_call_target="tpu_custom_call" | custom-call | flops 10000000000 | bytes 20000000 | tf_op jit(solution)/shard_map/pallas_call | solution.py:487
  68.1 0.0 copy-done
  68.1 0.6 copy.15
  68.7 0.0 copy-done.1
  68.7 0.5 copy.16
Async XLA Ops:
  56.4 11.7 %copy-start = (bf16[8,3072]{1,0:T(8,128)(2,1)S(1)}, bf16[8,3072]{1,0:T(8,128)(2,1)}, u32[]{:S(2)}) copy-start(bf16[8,3072]{1,0:T(8,128)(2,1)} %get-tuple-element.26) | copy-start | bytes 147460
  56.4 12.3 %copy-start.1 = (f32[1,16]{1,0:T(1,128)S(1)}, f32[1,16]{1,0:T(1,128)}, u32[]{:S(2)}) copy-start(f32[1,16]{1,0:T(1,128)} %get-tuple-element.29) | copy-start | bytes 196

commit v5 on v4

--- a/solution.py
+++ b/solution.py
@@ -12,7 +12,7 @@
 MESH = pl.DeviceIdType.MESH
 DP, MP = 8, 16
 SLICES, COLS = 6, 256
-ORDERS = (("x", "y", "z"), ("z", "x", "y"), ("y", "z", "x"))
+FLOWS = ((0, "xyz"), (1, "zxy"), (2, "yzx"))
 SWAP, RING, PLANE, X_SUM, OUT_SUM, COT, BACK, X_DP, COEF = 0, 1, 28, 40, 48, 56, 64, 72, 76
 COPIES = COEF + MP - 1
 
@@ -144,19 +144,19 @@
     here = {"z": z, "y": y, "x": x}
     nexts = {"z": (z_next, z_last, z_far), "y": (y_next, y_last, y_peer), "x": (x_next, x_last, x_far)}
 
-    def region(o, stage, by, whose):
-        order = ORDERS[o]
+    def region(o, stage, by, whose, ref=cots):
+        order = FLOWS[o][1]
         index = dict(here)
         for a in order[:stage]:
             index[a] = slice(None)
         index[order[stage]] = (here[order[stage]] + by) % 4
-        return cots.at[3 * whose + o, index["z"], index["y"], index["x"]]
-
-    def ring_send(stage):
-        for o in range(3):
+        return ref.at[3 * whose + o, index["z"], index["y"], index["x"]]
+
+    def ring_send(stage, which=(0, 1, 2), ways=(0, 1, 2)):
+        for o in which:
             ref = region(o, stage, 0, core)
-            for i, to in enumerate(nexts[ORDERS[o][stage]]):
-                send(RING + (o * 3 + stage) * 3 + i, ref, ref, to)
+            for i in ways:
+                send(RING + (o * 3 + stage) * 3 + i, ref, ref, nexts[FLOWS[o][1][stage]][i])
 
     def ring_arrive(o, stage, i):
         arrive(RING + (o * 3 + stage) * 3 + i, region(o, stage, (3, 1, 2)[i], core))
@@ -166,12 +166,20 @@
             for i in range(3):
                 ring_arrive(o, stage, i)
 
+    stores = []
+
+    def store(src, dst):
+        copy = pltpu.make_async_copy(src, dst, store_sem.at[len(stores)])
+        copy.start()
+        stores.append(copy)
+
     def plane_send(o, by):
-        ref = region(o, 2, by, core)
-        send(PLANE + o * 4 + by, ref, ref, sibling)
+        src, dst = region(o, 2, by, core), region(o, 2, by, core, cot_hbm)
+        send(PLANE + o * 4 + by, src, dst, sibling)
+        store(src, dst)
 
     def plane_arrive(o, by):
-        arrive(PLANE + o * 4 + by, region(o, 2, by, other))
+        arrive(PLANE + o * 4 + by, region(o, 2, by, other, cot_hbm))
 
     low = 1 - y_hi
     along = ((x_next, ahead), (x_last, behind), (x_far, far))
@@ -225,6 +233,8 @@
         arrive(base + 7, ref.at[:, :, other])
 
     gather_first(COT, crystal)
+    arrive(SWAP, cots.at[pl.ds(3 * core, 3), z, y, x, other])
+    ring_send(0)
 
     feats_copy.wait()
     group = 4
@@ -240,10 +250,10 @@
 
     span(0, width // block, spread_block)
     sum_cores(X_SUM, x_parts, x_pair)
-    arrive(SWAP, cots.at[pl.ds(3 * core, 3), z, y, x, other])
-    ring_send(0)
     sum_x(X_SUM, x_parts, x_pair, x_held, x_slots)
     gather_second(COT, crystal)
+    ring_all(0)
+    ring_send(1)
 
     def merge(t):
         weight_copy(t).wait()
@@ -252,19 +262,12 @@
             total += coefs_ref[d, k] * weights[t, k].astype(F32)
         merged[:, pl.ds(pl.multiple_of(t * LANES, LANES), LANES)] = total.astype(BF16)
 
-    span(0, tiles // 3, merge)
-    ring_all(0)
-    ring_send(1)
+    span(0, 2 * tiles // 3, merge)
     sum_y(X_SUM, x_held, x_slots, x_cross)
-    span(tiles // 3, 2 * tiles // 3, merge)
+    span(2 * tiles // 3, tiles, merge)
+    ring_all(1)
+    ring_send(2, (0,))
     gather_cores(COT, crystal)
-    span(2 * tiles // 3, tiles, merge)
-
-    gather_end(COT, crystal)
-    by_real, by_imag = separate(wide, dot(merged[...], crystal[...].reshape(-1, width), ((1,), (1,))))
-    back_all[y_hi, x, core] = (by_real + turn(by_imag)).astype(BF16)
-    gather_first(BACK, back_all)
-
     x_here = sum_end(X_SUM, x_held, x_slots, x_cross).astype(BF16)
     x_all[d] = x_here
     send(X_DP, x_all.at[d], x_all.at[d], lo_peer)
@@ -282,12 +285,16 @@
     span(0, width // block, out_block)
     sum_cores(OUT_SUM, out_parts, out_pair)
 
-    ring_all(1)
-    ring_send(2)
+    gather_end(COT, crystal)
+    by_real, by_imag = separate(wide, dot(merged[...], crystal[...].reshape(-1, width), ((1,), (1,))))
+    back_all[y_hi, x, core] = (by_real + turn(by_imag)).astype(BF16)
+    gather_first(BACK, back_all)
+    sum_x(OUT_SUM, out_parts, out_pair, out_held, out_slots)
+    ring_send(2, (1,), (0, 1))
+    gather_second(BACK, back_all)
+    ring_send(2, (2,))
     for o in range(3):
         plane_send(o, 0)
-    gather_second(BACK, back_all)
-    sum_x(OUT_SUM, out_parts, out_pair, out_held, out_slots)
     pair = x_all.at[pl.ds(2 * z, 2)]
     arrive(X_DP, x_all.at[d + 1 - 2 * y_lo])
     for i, to in enumerate((z_next, z_last, z_far)):
@@ -305,6 +312,7 @@
     sums = tuple(jnp.zeros((8, LANES), F32) for _ in range(experts))
     sums = lax.fori_loop(0, tiles // 2, coef_add, sums)
     sum_y(OUT_SUM, out_held, out_slots, out_cross)
+    ring_send(2, (1,), (2,))
     sums = lax.fori_loop(tiles // 2, tiles, coef_add, sums)
     lanes = jnp.sum(jnp.concatenate([jnp.sum(v, 0, keepdims=True) for v in sums], 0), 1, keepdims=True)
     same = lax.broadcasted_iota(jnp.int32, (experts, LANES), 0) == lax.broadcasted_iota(
@@ -338,13 +346,6 @@
         rows_of = x_all[i].astype(F32)
         both_all[i] = interleave(wide, rows_of, -turn(rows_of)).astype(BF16)
 
-    stores = []
-
-    def store(src, dst):
-        copy = pltpu.make_async_copy(src, dst, store_sem.at[len(stores)])
-        copy.start()
-        stores.append(copy)
-
     store(both_all, both_hbm)
     gather_end(BACK, back_all)
     store(back_all, back_hbm)
@@ -352,20 +353,12 @@
         for o in range(3):
             ring_arrive(o, 2, i)
             plane_send(o, by)
-    for o in range(3):
-        store(cots.at[3 * core + o], cot_hbm.at[3 * core + o])
-
     span(1, MP, lambda j: coef_copy(j).wait_recv())
     coef_ref[...] = jnp.sum(coef_parts[...], 0)[:, :experts] * (width**-0.5)
 
     for by in (0, 3, 1, 2):
         for o in range(3):
             plane_arrive(o, by)
-            index = [slice(None)] * 3
-            axis = "zyx".index(ORDERS[o][2])
-            index[axis] = (here["zyx"[axis]] + by) % 4
-            at = (3 * other + o, *index)
-            store(cots.at[at], cot_hbm.at[at])
 
     span(1, MP, lambda j: coef_copy(j).wait_send())
     for copy in sent:
@@ -416,7 +409,7 @@
             pltpu.VMEM((MP, 1, LANES), F32),
             pltpu.VMEM((2, 2 * rows, LANES), F32),
             *sums,
-            dma(()), dma((width // LANES,)), dma((17,)), dma((COPIES,)), dma((COPIES,)),
+            dma(()), dma((width // LANES,)), dma((14,)), dma((COPIES,)), dma((COPIES,)),
         ],
         compiler_params=pltpu.CompilerParams(
             collective_id=0, has_side_effects=True, vmem_limit_bytes=56 * 2**20

time: 69.5 us -> 67 us (0.964)
  Pallas kernels: 66.7 us -> 64.2 us
    pallas_call x1, Pallas kernels: 55.1 us -> 52.6 us  [exchange(): pl.pallas_call(functools.partial(exchange_kernel, (atoms_here / slots) **...]
where the time goes in v5:
time: 67 us; the launch traced here: 66.7 us
  Pallas kernels  64.2 us (96%)
  between operations  1.32 us (2%)
  local copies, waits for them, and re-layouts  1.14 us (2%)
    pallas_call x1, Pallas kernels, exchange(): pl.pallas_call(functools.partial(exchange_kernel, (atoms_here / slots) **...  52.6 us
    pallas_call x1, Pallas kernels, mix(): pl.pallas_call(functools.partial(mix_kernel, norm), grid=(SLICES,), in_sp...  11.6 us

profile of v5, /device:TPU:1, one launch (start us, length us, event | category | flops | bytes accessed | tf_op | source)
XLA Modules:
  0.0 66.7 jit_solution(15140571976296857330)
XLA Ops:
  1.3 52.6 %shard_map.111 = (bf16[8,3072]{1,0:T(8,128)(2,1)}, f32[1,16]{1,0:T(1,128)}, bf16[2,256,256]{2,1,0:T(8,128)(2,1)}, bf16[512,256]{1,0:T(8,128)(2,1)}, bf16[8,192,2...) custom-call(bf16[256,3072]{1,0:T(8,128)(2,1)} %feats_hbm.1, ...), custom_call_target="tpu_custom_call" | custom-call | flops 4000000000 | bytes 20000000 | tf_op jit(solution)/shard_map/pallas_call | solution.py:386
  53.8 0.0 copy-start
  53.9 0.0 copy-start.1
  53.9 11.6 %shard_map.112 = (bf16[16,96,2,1536]{3,2,1,0:T(2,128)(2,1)}, bf16[256,3072]{1,0:T(8,128)(2,1)}) custom-call(bf16[512,256]{1,0:T(8,128)(2,1)} %get-tuple-element.14.left_ref, bf16[8,192,256]{2,1,0:T(8,128)(2,1)} %get-tuple-element.15.both_ref, bf16[6,4,4,4,2,16,256]{6,5,4,3,2,1,0:T(8,128)(2,1)} %get-tuple-element.16.cot_ref, bf16[1536,256]{1,0:T(8,128)(2,1)} %bitcast.7, ...), custom_call_target="tpu_custom_call" | custom-call | flops 10000000000 | bytes 20000000 | tf_op jit(solution)/shard_map/pallas_call | solution.py:480
  65.5 0.0 copy-done
  65.5 0.6 copy.15
  66.1 0.0 copy-done.1
  66.1 0.5 copy.16
Async XLA Ops:
  53.8 11.7 %copy-start = (bf16[8,3072]{1,0:T(8,128)(2,1)S(1)}, bf16[8,3072]{1,0:T(8,128)(2,1)}, u32[]{:S(2)}) copy-start(bf16[8,3072]{1,0:T(8,128)(2,1)} %get-tuple-element.26) | copy-start | bytes 147460
  53.9 12.3 %copy-start.1 = (f32[1,16]{1,0:T(1,128)S(1)}, f32[1,16]{1,0:T(1,128)}, u32[]{:S(2)}) copy-start(f32[1,16]{1,0:T(1,128)} %get-tuple-element.29) | copy-start | bytes 196

commit v6 on v5

--- a/solution.py
+++ b/solution.py
@@ -14,7 +14,8 @@
 SLICES, COLS = 6, 256
 FLOWS = ((0, "xyz"), (1, "zxy"), (2, "yzx"))
 SWAP, RING, PLANE, X_SUM, OUT_SUM, COT, BACK, X_DP, COEF = 0, 1, 28, 40, 48, 56, 64, 72, 76
-COPIES = COEF + MP - 1
+RELAY = COEF + MP - 1
+COPIES = RELAY + 6
 
 
 def dot(a, b, contract):
@@ -144,12 +145,14 @@
     here = {"z": z, "y": y, "x": x}
     nexts = {"z": (z_next, z_last, z_far), "y": (y_next, y_last, y_peer), "x": (x_next, x_last, x_far)}
 
-    def region(o, stage, by, whose, ref=cots):
+    def region(o, stage, by, whose, ref=cots, half=None):
         order = FLOWS[o][1]
         index = dict(here)
         for a in order[:stage]:
             index[a] = slice(None)
         index[order[stage]] = (here[order[stage]] + by) % 4
+        if half is not None:
+            index["y" if order[stage] == "z" else "z"] = slice(2 * half, 2 * half + 2)
         return ref.at[3 * whose + o, index["z"], index["y"], index["x"]]
 
     def ring_send(stage, which=(0, 1, 2), ways=(0, 1, 2)):
@@ -160,6 +163,18 @@
 
     def ring_arrive(o, stage, i):
         arrive(RING + (o * 3 + stage) * 3 + i, region(o, stage, (3, 1, 2)[i], core))
+
+    def ring_relay(o):
+        for h, by in ((0, 3), (1, 1)):
+            ring_arrive(o, 2, h)
+            ref = region(o, 2, by, core, half=h)
+            send(RELAY + 2 * o + h, ref, ref, nexts[FLOWS[o][1][2]][h])
+            plane_send(o, by)
+
+    def ring_end(o):
+        for h in range(2):
+            arrive(RELAY + 2 * o + h, region(o, 2, 2, core, half=h))
+        plane_send(o, 2)
 
     def ring_all(stage):
         for o in range(3):
@@ -266,7 +281,7 @@
     sum_y(X_SUM, x_held, x_slots, x_cross)
     span(2 * tiles // 3, tiles, merge)
     ring_all(1)
-    ring_send(2, (0,))
+    ring_send(2, (0,), (0, 1))
     gather_cores(COT, crystal)
     x_here = sum_end(X_SUM, x_held, x_slots, x_cross).astype(BF16)
     x_all[d] = x_here
@@ -292,7 +307,8 @@
     sum_x(OUT_SUM, out_parts, out_pair, out_held, out_slots)
     ring_send(2, (1,), (0, 1))
     gather_second(BACK, back_all)
-    ring_send(2, (2,))
+    ring_send(2, (2,), (0, 1))
+    ring_relay(0)
     for o in range(3):
         plane_send(o, 0)
     pair = x_all.at[pl.ds(2 * z, 2)]
@@ -312,7 +328,7 @@
     sums = tuple(jnp.zeros((8, LANES), F32) for _ in range(experts))
     sums = lax.fori_loop(0, tiles // 2, coef_add, sums)
     sum_y(OUT_SUM, out_held, out_slots, out_cross)
-    ring_send(2, (1,), (2,))
+    ring_relay(1)
     sums = lax.fori_loop(tiles // 2, tiles, coef_add, sums)
     lanes = jnp.sum(jnp.concatenate([jnp.sum(v, 0, keepdims=True) for v in sums], 0), 1, keepdims=True)
     same = lax.broadcasted_iota(jnp.int32, (experts, LANES), 0) == lax.broadcasted_iota(
@@ -327,6 +343,7 @@
     span(1, MP, lambda j: coef_copy(j).start())
 
     gather_cores(BACK, back_all)
+    ring_relay(2)
 
     r = lax.broadcasted_iota(jnp.int32, (32, 32 * DP), 0)
     c = lax.broadcasted_iota(jnp.int32, (32, 32 * DP), 1)
@@ -349,10 +366,9 @@
     store(both_all, both_hbm)
     gather_end(BACK, back_all)
     store(back_all, back_hbm)
-    for i, by in enumerate((3, 1, 2)):
-        for o in range(3):
-            ring_arrive(o, 2, i)
-            plane_send(o, by)
+    for o in range(3):
+        ring_end(o)
+
     span(1, MP, lambda j: coef_copy(j).wait_recv())
     coef_ref[...] = jnp.sum(coef_parts[...], 0)[:, :experts] * (width**-0.5)
 

time: 67 us -> 65.7 us (0.981)
  Pallas kernels: 64.2 us -> 62.9 us
    pallas_call x1, Pallas kernels: 52.6 us -> 51.3 us  [exchange(): pl.pallas_call(functools.partial(exchange_kernel, (atoms_here / slots) **...]
where the time goes in v6:
time: 65.7 us; the launch traced here: 65.3 us
  Pallas kernels  62.9 us (96%)
  between operations  1.32 us (2%)
  local copies, waits for them, and re-layouts  1.14 us (2%)
    pallas_call x1, Pallas kernels, exchange(): pl.pallas_call(functools.partial(exchange_kernel, (atoms_here / slots) **...  51.3 us
    pallas_call x1, Pallas kernels, mix(): pl.pallas_call(functools.partial(mix_kernel, norm), grid=(SLICES,), in_sp...  11.6 us

profile of v6, /device:TPU:1, one launch (start us, length us, event | category | flops | bytes accessed | tf_op | source)
XLA Modules:
  0.0 65.3 jit_solution(4720156731850367986)
XLA Ops:
  1.3 51.3 %shard_map.111 = (bf16[8,3072]{1,0:T(8,128)(2,1)}, f32[1,16]{1,0:T(1,128)}, bf16[2,256,256]{2,1,0:T(8,128)(2,1)}, bf16[512,256]{1,0:T(8,128)(2,1)}, bf16[8,192,2...) custom-call(bf16[256,3072]{1,0:T(8,128)(2,1)} %feats_hbm.1, ...), custom_call_target="tpu_custom_call" | custom-call | flops 4000000000 | bytes 20000000 | tf_op jit(solution)/shard_map/pallas_call | solution.py:402
  52.5 0.0 copy-start
  52.5 0.0 copy-start.1
  52.6 11.6 %shard_map.112 = (bf16[16,96,2,1536]{3,2,1,0:T(2,128)(2,1)}, bf16[256,3072]{1,0:T(8,128)(2,1)}) custom-call(bf16[512,256]{1,0:T(8,128)(2,1)} %get-tuple-element.14.left_ref, bf16[8,192,256]{2,1,0:T(8,128)(2,1)} %get-tuple-element.15.both_ref, bf16[6,4,4,4,2,16,256]{6,5,4,3,2,1,0:T(8,128)(2,1)} %get-tuple-element.16.cot_ref, bf16[1536,256]{1,0:T(8,128)(2,1)} %bitcast.7, ...), custom_call_target="tpu_custom_call" | custom-call | flops 10000000000 | bytes 20000000 | tf_op jit(solution)/shard_map/pallas_call | solution.py:496
  64.2 0.0 copy-done
  64.2 0.6 copy.15
  64.8 0.0 copy-done.1
  64.8 0.5 copy.16
Async XLA Ops:
  52.5 11.7 %copy-start = (bf16[8,3072]{1,0:T(8,128)(2,1)S(1)}, bf16[8,3072]{1,0:T(8,128)(2,1)}, u32[]{:S(2)}) copy-start(bf16[8,3072]{1,0:T(8,128)(2,1)} %get-tuple-element.26) | copy-start | bytes 147460
  52.5 12.3 %copy-start.1 = (f32[1,16]{1,0:T(1,128)S(1)}, f32[1,16]{1,0:T(1,128)}, u32[]{:S(2)}) copy-start(f32[1,16]{1,0:T(1,128)} %get-tuple-element.29) | copy-start | bytes 196

commit v7 on v6

--- a/solution.py
+++ b/solution.py
@@ -436,7 +436,13 @@
     )
 
 
-def mix_kernel(norm, left_ref, both_ref, cot_ref, back_ref, spread_ref, wg_hbm, eg_ref, gm_ref, out_ref, sem):
+def mix_kernel(norm, left_ref, both_ref, cot_ref, back_ref, spread_ref, atom_in, coef_in, wg_hbm, eg_ref, atom_ref,
+               coef_ref, gm_ref, out_ref, sem):
+    @pl.when(pl.program_id(0) == 0)
+    def _():
+        atom_ref[...] = atom_in[...]
+        coef_ref[...] = coef_in[...]
+
     step, steps = pl.program_id(0), pl.num_programs(0)
     crystals, double, _ = both_ref.shape
     experts, _, _, width = wg_hbm.shape
@@ -488,7 +494,7 @@
             copy.wait()
 
 
-def mix(experts, left, both_all, cot_all, back_all, spread, norm):
+def mix(experts, left, both_all, cot_all, back_all, spread, atom_out, coef_grad, norm):
     crystals, double, _ = both_all.shape
     width = back_all.shape[0]
     slots = spread.shape[1]
@@ -502,14 +508,20 @@
             pl.BlockSpec((1,) + cot_all.shape[1:], lambda i: (i,) + (0,) * 6),
             whole(back_all.shape),
             whole(spread.shape),
+            whole(atom_out.shape),
+            whole(coef_grad.shape),
         ],
         out_specs=[
             pl.BlockSpec(memory_space=pl.ANY),
             pl.BlockSpec((slots, 2 * width // SLICES), lambda i: (0, i)),
+            whole(atom_out.shape),
+            whole(coef_grad.shape),
         ],
         out_shape=[
             jax.ShapeDtypeStruct((experts, double // 2, 2, width), BF16),
             jax.ShapeDtypeStruct((slots, 2 * width), BF16),
+            jax.ShapeDtypeStruct(atom_out.shape, BF16),
+            jax.ShapeDtypeStruct(coef_grad.shape, F32),
         ],
         scratch_shapes=[
             pltpu.VMEM((crystals, double, COLS), BF16),
@@ -518,7 +530,7 @@
         ],
         compiler_params=pltpu.CompilerParams(vmem_limit_bytes=60 * 2**20),
         cost_estimate=pl.CostEstimate(flops=10**10, bytes_accessed=2 * 10**7, transcendentals=0),
-    )(left, both_all, cot_all, back_all, spread)
+    )(left, both_all, cot_all, back_all, spread, atom_out, coef_grad)
 
 
 def on_device(edge_feats, targets, roll_ids, counts, coefs, weights, roll_angles, atom_cot):
@@ -527,8 +539,8 @@
         edge_feats, targets, roll_ids, counts, coefs, weights, roll_angles, atom_cot
     )
     back_all = back_all.reshape(-1, back_all.shape[-1])
-    weight_grad, edge_grad = mix(
-        weights.shape[0], left, both_all, cot_all, back_all, spread, (slots * MP) ** -0.5
+    weight_grad, edge_grad, atom_out, coef_grad = mix(
+        weights.shape[0], left, both_all, cot_all, back_all, spread, atom_out, coef_grad, (slots * MP) ** -0.5
     )
     return (atom_out, edge_grad, weight_grad, coef_grad)
 

time: 65.7 us -> 64.5 us (0.982)
  local copies, waits for them, and re-layouts: 1.14 us -> 0 us
    unnamed x6 -> x0, local copies, waits for them, and re-layouts: 1.14 us -> none
where the time goes in v7:
time: 64.5 us; the launch traced here: 64.2 us
  Pallas kernels  62.9 us (98%)
  between operations  1.29 us (2%)
    pallas_call x1, Pallas kernels, exchange(): pl.pallas_call(functools.partial(exchange_kernel, (atoms_here / slots) **...  51.2 us
    pallas_call x1, Pallas kernels, mix(): pl.pallas_call(functools.partial(mix_kernel, norm), grid=(SLICES,), in_sp...  11.7 us

profile of v7, /device:TPU:1, one launch (start us, length us, event | category | flops | bytes accessed | tf_op | source)
XLA Modules:
  0.0 64.2 jit_solution(2095163833002152441)
XLA Ops:
  1.3 51.2 %shard_map.111 = (bf16[8,3072]{1,0:T(8,128)(2,1)}, f32[1,16]{1,0:T(1,128)}, bf16[2,256,256]{2,1,0:T(8,128)(2,1)}, bf16[512,256]{1,0:T(8,128)(2,1)}, bf16[8,192,2...) custom-call(bf16[256,3072]{1,0:T(8,128)(2,1)} %feats_hbm.1, ...), custom_call_target="tpu_custom_call" | custom-call | flops 4000000000 | bytes 20000000 | tf_op jit(solution)/shard_map/pallas_call | solution.py:402
  52.5 11.7 %shard_map.112 = (bf16[16,96,2,1536]{3,2,1,0:T(2,128)(2,1)}, bf16[256,3072]{1,0:T(8,128)(2,1)}, bf16[8,3072]{1,0:T(8,128)(2,1)}, f32[1,16]{1,0:T(1,128)}) custom-call(bf16[512,256]{1,0:T(8,128)(2,1)} %get-tuple-element.15.left_ref, bf16[8,192,256]{2,1,0:T(8,128)(2,1)} %get-tuple-element.16.both_ref, ...), custom_call_target="tpu_custom_call" | custom-call | flops 10000000000 | bytes 20000000 | tf_op jit(solution)/shard_map/pallas_call | solution.py:502
